TPU v7x, 512 devices: a whole 4x4x16 slice. The times are simulated.
512 devices in a mesh: ctx: 128 (over z, y, core), head: 4 (over x).
Axes of the slice: x: 4, y: 4, z: 16, core: 2. Of those that a mesh axis runs over, the one named last changes fastest.
Arguments:
- queries: bfloat16 [16384, 4096], P(('ctx', 'head')), may hold values from -24 to 24
- key_rows: bfloat16 [16384, 4096], P(('ctx', 'head')), may hold values from -12 to 12
- value_rows: bfloat16 [16384, 4096], P(('ctx', 'head')), may hold values from -6 to 6
- rel_bias: float32 [32, 32], P(None, 'head'), may hold values from -4 to 4
- offsets: int32 [2, 32], P(None, 'head'), may hold values from 0 to 63, as said below
Outputs:
- attended: bfloat16 [16384, 4096], P(('ctx', 'head'))
Inputs may be any that keep to these rules, and one draw needn't show every extreme that they name: offsets[0, h] is below 4 and offsets[1, h] is below 64.
All inputs are finite; a program needn't handle non-finite values.
Results may differ from a plain program's by a relative error of at most 0.005.
Values may be sent and summed in bfloat16 or wider, within the bound.
No kernel may reach another device: no remote copies, remote signals or barrier semaphores. Data moves between devices by JAX's collectives and lax.ppermute only.
A program may use at most 64 MiB of HBM per device.

v0:
```python
import math

import jax
import jax.numpy as jnp
from jax import lax
from jax.sharding import PartitionSpec as P

DH = 128
BUCKETS = 32
MAXDIST = 128
R1 = 4
SPAN = 256


def shifted(block, axis, distance):
    devices = range(lax.axis_size(axis))
    route = [(i - distance, i) for i in devices if i - distance in devices]
    return lax.ppermute(block, axis, route)


def bucket_edges():
    half_count = BUCKETS // 2
    thresholds = []
    for target in range(half_count + 1, BUCKETS):
        thresholds.append(
            int(
                math.ceil(
                    half_count * (MAXDIST / half_count) ** ((target - half_count) / half_count)
                )
            )
        )
    return thresholds


def bucket_of(token_separation):
    half_count = BUCKETS // 2
    far_bucket = jnp.full(token_separation.shape, half_count, jnp.int32)
    for border in bucket_edges():
        far_bucket = far_bucket + (token_separation >= border).astype(jnp.int32)
    return jnp.where(token_separation < half_count, token_separation, far_bucket)


def bias_block(position_bias_lookup, ask_count, key_count, advance, stride):
    ask_spots = jnp.arange(ask_count, dtype=jnp.int32)[:, None]
    key_spots = jnp.arange(key_count, dtype=jnp.int32)[None, :]
    token_separation = jnp.maximum((ask_spots - key_spots + advance) * stride, 0)
    bucket_grid = bucket_of(token_separation)
    indicator_matrix = (
        jnp.arange(BUCKETS, dtype=jnp.int32)[:, None, None] == bucket_grid[None]
    ).astype(jnp.float32)
    return jnp.einsum(
        "lnd,lc->cnd", indicator_matrix, position_bias_lookup, precision=lax.Precision.HIGHEST
    )


def start_state(ask_count, n_heads):
    return (
        jnp.full((n_heads, ask_count), -1e30, jnp.float32),
        jnp.zeros((n_heads, ask_count), jnp.float32),
        jnp.zeros((ask_count, n_heads, DH), jnp.float32),
    )


def attend(running, asks, key_part, value_part, advance, stride, position_bias_lookup, usable):
    ask_count = asks.shape[0]
    key_count = key_part.shape[0]
    scores = jnp.einsum(
        "qhd,khd->hqk", asks, key_part, preferred_element_type=jnp.float32
    ) * asks.shape[2] ** (-0.5)
    scores = scores + bias_block(position_bias_lookup, ask_count, key_count, advance, stride)
    allowed = (
        jnp.arange(ask_count, dtype=jnp.int32)[:, None] + advance
        >= jnp.arange(key_count, dtype=jnp.int32)[None, :]
    ) & usable
    held = jnp.where(allowed[None], scores, -1e30)
    row_top, row_sum, row_acc = running
    fresh = jnp.maximum(row_top, jnp.max(held, axis=2))
    weights = jnp.where(allowed[None], jnp.exp(held - fresh[:, :, None]), 0.0)
    shrink = jnp.exp(row_top - fresh)
    row_sum = row_sum * shrink + jnp.sum(weights, axis=2)
    blended = jnp.einsum(
        "hqk,khd->qhd", weights.astype(jnp.bfloat16), value_part, preferred_element_type=jnp.float32
    )
    row_acc = row_acc * jnp.transpose(shrink)[:, :, None] + blended
    return (fresh, row_sum, row_acc)


def finish(running):
    row_top, row_sum, row_acc = running
    result = (row_acc / jnp.transpose(row_sum)[:, :, None]).astype(jnp.bfloat16)
    return (result, jnp.transpose(row_top + jnp.log(row_sum)))


def select_rows(tokens, picks, stride):
    n_rows, n_heads, head_dim = tokens.shape
    grouped = tokens.reshape(n_rows // stride, stride, n_heads, head_dim)
    wanted = jnp.arange(stride, dtype=jnp.int32)[None, :, None, None] == picks[None, None, :, None]
    picked = jnp.where(wanted, grouped, jnp.zeros((), tokens.dtype))
    return jnp.sum(picked, axis=1, dtype=tokens.dtype)


def merge_block(
    first_out, leading_logsumexp, mid_out, mid_lse, far_out, far_lse, mid_pick, far_pick
):
    long_rate = first_out.shape[1]
    spots = jnp.arange(long_rate, dtype=jnp.int32)[:, None]
    mid_cover = (spots % R1 == mid_pick[None, :])[None]
    far_cover = (spots == far_pick[None, :])[None]
    mid_lse_wide = jnp.repeat(mid_lse, R1, axis=1)
    mid_out_wide = jnp.repeat(mid_out, R1, axis=1)
    far_lse_wide = jnp.broadcast_to(far_lse[:, None, :], leading_logsumexp.shape)
    peak = jnp.maximum(
        leading_logsumexp,
        jnp.maximum(
            jnp.where(mid_cover, mid_lse_wide, leading_logsumexp),
            jnp.where(far_cover, far_lse_wide, leading_logsumexp),
        ),
    )
    first_weight = jnp.exp(leading_logsumexp - peak)
    mid_weight = jnp.where(mid_cover, jnp.exp(jnp.where(mid_cover, mid_lse_wide, peak) - peak), 0.0)
    far_weight = jnp.where(far_cover, jnp.exp(jnp.where(far_cover, far_lse_wide, peak) - peak), 0.0)
    blended = (
        first_weight[..., None] * first_out.astype(jnp.float32)
        + mid_weight[..., None] * mid_out_wide.astype(jnp.float32)
        + far_weight[..., None] * far_out[:, None].astype(jnp.float32)
    )
    return (blended / (first_weight + mid_weight + far_weight)[..., None]).astype(jnp.bfloat16)


def nearby_dilation_period(running, asks, moving, kept, position_bias_lookup, position, group):
    tok_rows = asks.shape[0]

    def near_turn(turn_no, carried):
        current_state_value, moving_now, kept_now = carried
        moving_now = shifted(moving_now, "ctx", 1)
        current_state_value = attend(
            current_state_value,
            asks,
            moving_now[0],
            moving_now[1],
            turn_no * tok_rows,
            1,
            position_bias_lookup,
            position >= turn_no,
        )
        return (current_state_value, moving_now, kept_now)

    result = lax.fori_loop(1, group, near_turn, (running, moving, kept))
    return (result[0], result[2])


def mid_cycle(running, asks, moving, position_bias_lookup, position, from_turn, group):
    mid_rows = asks.shape[0]

    def mid_turn(turn_no, carried):
        current_state_value, moving_now = carried
        moving_now = shifted(moving_now, "ctx", 1)
        current_state_value = attend(
            current_state_value,
            asks,
            moving_now[0],
            moving_now[1],
            turn_no * mid_rows,
            R1,
            position_bias_lookup,
            position >= turn_no,
        )
        return (current_state_value, moving_now)

    return lax.fori_loop(from_turn, group, mid_turn, (running, moving))[0]


def on_device(queries, key_rows, value_rows, rel_bias, offsets):
    local_q, local_k, local_v = (
        lax.all_to_all(queries, "head", split_axis=1, concat_axis=0, tiled=True),
        lax.all_to_all(key_rows, "head", split_axis=1, concat_axis=0, tiled=True),
        lax.all_to_all(value_rows, "head", split_axis=1, concat_axis=0, tiled=True),
    )
    tok_rows = local_q.shape[0]
    n_heads = rel_bias.shape[1]
    asks = local_q.reshape(tok_rows, n_heads, DH)
    keys_here = local_k.reshape(tok_rows, n_heads, DH)
    vals_here = local_v.reshape(tok_rows, n_heads, DH)
    n_ctx = lax.axis_size("ctx")
    place = lax.axis_index("ctx")
    long_rate = tok_rows * n_ctx // SPAN
    near_group = SPAN // tok_rows
    mid_rows = tok_rows // R1
    mid_group = R1 * SPAN // tok_rows
    far_rows = tok_rows // long_rate
    mid_pick = offsets[0]
    far_pick = offsets[1]
    mid_q = select_rows(asks, mid_pick, R1)
    mid_k = select_rows(keys_here, mid_pick, R1)
    mid_v = select_rows(vals_here, mid_pick, R1)
    mid_pair = jnp.stack([mid_k, mid_v])
    first_state = attend(
        start_state(tok_rows, n_heads), asks, keys_here, vals_here, 0, 1, rel_bias, True
    )
    first_state, kept = nearby_dilation_period(
        first_state,
        asks,
        jnp.stack([keys_here, vals_here]),
        mid_pair,
        rel_bias,
        place % near_group,
        near_group,
    )
    mid_state = attend(start_state(mid_rows, n_heads), mid_q, mid_k, mid_v, 0, R1, rel_bias, True)
    mid_state = mid_cycle(mid_state, mid_q, mid_pair, rel_bias, place % mid_group, 1, mid_group)
    far_q = select_rows(asks, far_pick, long_rate)
    far_k = select_rows(keys_here, far_pick, long_rate)
    far_v = select_rows(vals_here, far_pick, long_rate)
    far_state = attend(
        start_state(far_rows, n_heads),
        far_q,
        lax.all_gather(far_k, "ctx", axis=0, tiled=True),
        lax.all_gather(far_v, "ctx", axis=0, tiled=True),
        place * far_rows,
        long_rate,
        rel_bias,
        True,
    )
    far_out, far_lse = finish(far_state)
    first_out, leading_logsumexp = finish(first_state)
    mid_out, mid_lse = finish(mid_state)
    merged = merge_block(
        first_out.reshape(far_rows, long_rate, n_heads, DH),
        leading_logsumexp.reshape(far_rows, long_rate, n_heads),
        mid_out.reshape(far_rows, long_rate // R1, n_heads, DH),
        mid_lse.reshape(far_rows, long_rate // R1, n_heads),
        far_out,
        far_lse,
        mid_pick,
        far_pick,
    )
    merged = merged.reshape(tok_rows, n_heads * DH)
    return lax.all_to_all(merged, "head", split_axis=0, concat_axis=1, tiled=True)


def solution(mesh):
    in_specs = (
        P(("ctx", "head"), None),
        P(("ctx", "head"), None),
        P(("ctx", "head"), None),
        P(None, "head"),
        P(None, "head"),
    )
    out_specs = P(("ctx", "head"), None)
    return jax.shard_map(
        on_device, mesh=mesh, in_specs=in_specs, out_specs=out_specs, check_vma=False
    )
```

profile of v0, /device:TPU:128, one launch (start us, length us, event | category | flops | bytes accessed | tf_op | source)
XLA Modules:
  0.0 295.4 jit_solution(1167431653436418967)
XLA Ops:
  0.0 1.7 copy.297
  1.7 4.3 %all-to-all-start = ((bf16[32,4,1024]{2,0,1:T(8,128)(2,1)}), bf16[32,4,1024]{2,0,1:T(8,128)(2,1)S(1)}, u32[]{:S(2)}, u32[]{:S(2)}) async-start(bf16[32,4,1024]{2,0,1:T(8,128)(2,1)} %bitcast.228), calls=%async_computation | async-start | bytes 524288 | tf_op jit(solution)/shard_map/all_to_all | solution.py:175
  6.5 0.3 fusion.53
  7.3 0.7 copy.296
  8.0 0.7 copy.295
  8.7 0.7 fusion.31
  9.7 0.7 fusion.30
  10.7 2.0 all-to-all-done
  12.7 3.4 %all-to-all-start.1 = ((bf16[32,4,1024]{2,0,1:T(8,128)(2,1)}), bf16[32,4,1024]{2,0,1:T(8,128)(2,1)S(1)}, u32[]{:S(2)}, u32[]{:S(2)}) async-start(bf16[32,4,1024]{2,0,1:T(8,128)(2,1)} %bitcast.227), calls=%async_computation.1 | async-start | bytes 524288 | tf_op jit(solution)/shard_map/all_to_all | solution.py:176
  16.1 6.6 %all-to-all-done.1 = bf16[32,4,1024]{2,0,1:T(8,128)(2,1)S(1)} async-done(((bf16[32,4,1024]{2,0,1:T(8,128)(2,1)}), bf16[32,4,1024]{2,0,1:T(8,128)(2,1)S(1)}, u32[]{:S(2)}, u32[]{:S(2)}) %all-to-all-start.1) | async-done | bytes 262176 | tf_op jit(solution)/shard_map/all_to_all | solution.py:176
  22.7 3.4 %all-to-all-start.2 = ((bf16[32,4,1024]{2,0,1:T(8,128)(2,1)}), bf16[32,4,1024]{2,0,1:T(8,128)(2,1)S(1)}, u32[]{:S(2)}, u32[]{:S(2)}) async-start(bf16[32,4,1024]{2,0,1:T(8,128)(2,1)} %bitcast.226), calls=%async_computation.2 | async-start | bytes 524288 | tf_op jit(solution)/shard_map/all_to_all | solution.py:177
  26.3 6.5 %all-to-all-done.2 = bf16[32,4,1024]{2,0,1:T(8,128)(2,1)S(1)} async-done(((bf16[32,4,1024]{2,0,1:T(8,128)(2,1)}), bf16[32,4,1024]{2,0,1:T(8,128)(2,1)S(1)}, u32[]{:S(2)}, u32[]{:S(2)}) %all-to-all-start.2) | async-done | bytes 262176 | tf_op jit(solution)/shard_map/all_to_all | solution.py:177
  33.2 0.3 select_reduce_fusion
  34.1 85.1 %all_gather.6 = bf16[256,8,128]{2,1,0:T(8,128)(2,1)S(1)} all-gather(bf16[2,8,128]{2,1,0:T(8,128)(2,1)S(1)} %reduce_sum.144), channel_id=1, replica_groups=mesh['ctx'=128,'head'=4] {'ctx'}, dimensions={0}, use_global_device_ids=true | all-gather | bytes 528384 | tf_op jit(solution)/shard_map/all_gather | solution.py:217
  119.2 0.3 fusion.180
  119.7 80.7 %all_gather.7 = bf16[256,8,128]{2,1,0:T(8,128)(2,1)S(1)} all-gather(bf16[2,8,128]{2,1,0:T(8,128)(2,1)S(1)} %reduce_sum.149), channel_id=1, replica_groups=mesh['ctx'=128,'head'=4] {'ctx'}, dimensions={0}, use_global_device_ids=true | all-gather | bytes 528384 | tf_op jit(solution)/shard_map/all_gather | solution.py:218
  200.7 2.4 collective-permute-start.1
  203.2 74.2 %while.4 = (s32[]{:T(128)}, f32[8,32]{1,0:T(8,128)S(1)}, f32[8,32]{1,0:T(8,128)S(1)}, f32[32,8,128]{2,0,1:T(8,128)S(1)}, bf16[2,32,8,128]{3,1,2,0:T(8,128)(2,1)S...) while((s32[]{:T(128)}, f32[8,32]{1,0:T(8,128)S(1)}, ...), condition=%wide.region_12.13_spmd, body=%wide.region_9.12_spmd.sunk | while | flops 7575332 | bytes 1713579 | solution.py:170
  203.2 2.6 collective-permute-start
  205.9 0.3 fusion.194
  206.3 9.7 %collective-permute-done = bf16[2,32,8,128]{3,1,2,0:T(8,128)(2,1)S(1)} collective-permute-done((bf16[2,32,8,128]{3,1,2,0:T(8,128)(2,1)S(1)}, bf16[2,32,8,128]{3,1,2,0:T(8,128)(2,1)S(1)}, u32[]{:S(2)}, u32[]{:S(2)}) %collective-permute-start) | collective-permute-done | bytes 131104 | tf_op jit(solution)/shard_map/while/body/eval_jaxpr/ppermute | solution.py:18
  216.5 1.9 collective-permute-start
  218.5 0.3 fusion.194
  218.9 7.2 %collective-permute-done = bf16[2,32,8,128]{3,1,2,0:T(8,128)(2,1)S(1)} collective-permute-done((bf16[2,32,8,128]{3,1,2,0:T(8,128)(2,1)S(1)}, bf16[2,32,8,128]{3,1,2,0:T(8,128)(2,1)S(1)}, u32[]{:S(2)}, u32[]{:S(2)}) %collective-permute-start) | collective-permute-done | bytes 131104 | tf_op jit(solution)/shard_map/while/body/eval_jaxpr/ppermute | solution.py:18
  226.7 1.9 collective-permute-start
  228.6 0.3 fusion.194
  229.0 7.2 %collective-permute-done = bf16[2,32,8,128]{3,1,2,0:T(8,128)(2,1)S(1)} collective-permute-done((bf16[2,32,8,128]{3,1,2,0:T(8,128)(2,1)S(1)}, bf16[2,32,8,128]{3,1,2,0:T(8,128)(2,1)S(1)}, u32[]{:S(2)}, u32[]{:S(2)}) %collective-permute-start) | collective-permute-done | bytes 131104 | tf_op jit(solution)/shard_map/while/body/eval_jaxpr/ppermute | solution.py:18
  236.8 1.9 collective-permute-start
  238.8 0.3 fusion.194
  239.2 7.2 %collective-permute-done = bf16[2,32,8,128]{3,1,2,0:T(8,128)(2,1)S(1)} collective-permute-done((bf16[2,32,8,128]{3,1,2,0:T(8,128)(2,1)S(1)}, bf16[2,32,8,128]{3,1,2,0:T(8,128)(2,1)S(1)}, u32[]{:S(2)}, u32[]{:S(2)}) %collective-permute-start) | collective-permute-done | bytes 131104 | tf_op jit(solution)/shard_map/while/body/eval_jaxpr/ppermute | solution.py:18
  246.9 1.9 collective-permute-start
  248.9 0.3 fusion.194
  249.3 7.2 %collective-permute-done = bf16[2,32,8,128]{3,1,2,0:T(8,128)(2,1)S(1)} collective-permute-done((bf16[2,32,8,128]{3,1,2,0:T(8,128)(2,1)S(1)}, bf16[2,32,8,128]{3,1,2,0:T(8,128)(2,1)S(1)}, u32[]{:S(2)}, u32[]{:S(2)}) %collective-permute-start) | collective-permute-done | bytes 131104 | tf_op jit(solution)/shard_map/while/body/eval_jaxpr/ppermute | solution.py:18
  257.1 1.9 collective-permute-start
  259.1 0.3 fusion.194
  259.5 7.2 %collective-permute-done = bf16[2,32,8,128]{3,1,2,0:T(8,128)(2,1)S(1)} collective-permute-done((bf16[2,32,8,128]{3,1,2,0:T(8,128)(2,1)S(1)}, bf16[2,32,8,128]{3,1,2,0:T(8,128)(2,1)S(1)}, u32[]{:S(2)}, u32[]{:S(2)}) %collective-permute-start) | collective-permute-done | bytes 131104 | tf_op jit(solution)/shard_map/while/body/eval_jaxpr/ppermute | solution.py:18
  267.2 1.9 collective-permute-start
  269.2 0.3 fusion.194
  269.6 7.2 %collective-permute-done = bf16[2,32,8,128]{3,1,2,0:T(8,128)(2,1)S(1)} collective-permute-done((bf16[2,32,8,128]{3,1,2,0:T(8,128)(2,1)S(1)}, bf16[2,32,8,128]{3,1,2,0:T(8,128)(2,1)S(1)}, u32[]{:S(2)}, u32[]{:S(2)}) %collective-permute-start) | collective-permute-done | bytes 131104 | tf_op jit(solution)/shard_map/while/body/eval_jaxpr/ppermute | solution.py:18
  278.1 0.3 fusion.179
  278.4 1.3 fusion.178
  279.9 0.5 fusion.33
  280.4 1.3 fusion.42
  281.7 0.3 copy.223
  283.4 0.9 mul.193
  284.3 1.3 divide_convert_fusion
  285.6 9.1 %all_to_all.64 = bf16[4,32,1024]{2,1,0:T(8,128)(2,1)S(1)} all-to-all(bf16[4,32,1024]{2,1,0:T(8,128)(2,1)S(1)} %divide_convert_fusion), channel_id=1, replica_groups=mesh['ctx'=128,'head'=4] {'head'}, dimensions={0} | all-to-all | bytes 524288 | tf_op jit(solution)/shard_map/all_to_all | solution.py:238
  294.7 0.7 copy.240
  (157 shorter events, 9.6 us)
Async XLA Ops:
  0.0 6.3 %copy-start.3 = (s32[2,8]{1,0:T(2,128)S(1)}, s32[2,8]{1,0:T(2,128)}, u32[]{:S(2)}) copy-start(s32[2,8]{1,0:T(2,128)} %param.11) | copy-start | bytes 196
  0.0 6.3 %copy-start = (f32[32,8]{0,1:T(8,128)S(1)}, f32[32,8]{0,1:T(8,128)}, u32[]{:S(2)}) copy-start(f32[32,8]{0,1:T(8,128)} %param.10) | copy-start | bytes 3076
  1.7 11.0 %all-to-all-start = ((bf16[32,4,1024]{2,0,1:T(8,128)(2,1)}), bf16[32,4,1024]{2,0,1:T(8,128)(2,1)S(1)}, u32[]{:S(2)}, u32[]{:S(2)}) async-start(bf16[32,4,1024]{2,0,1:T(8,128)(2,1)} %bitcast.228), calls=%async_computation | async-start | bytes 524288 | tf_op jit(solution)/shard_map/all_to_all | solution.py:175
  6.0 1.3 copy-start.1
  6.9 1.1 copy-start.2
  12.7 10.1 %all-to-all-start.1 = ((bf16[32,4,1024]{2,0,1:T(8,128)(2,1)}), bf16[32,4,1024]{2,0,1:T(8,128)(2,1)S(1)}, u32[]{:S(2)}, u32[]{:S(2)}) async-start(bf16[32,4,1024]{2,0,1:T(8,128)(2,1)} %bitcast.227), calls=%async_computation.1 | async-start | bytes 524288 | tf_op jit(solution)/shard_map/all_to_all | solution.py:176
  22.7 10.1 %all-to-all-start.2 = ((bf16[32,4,1024]{2,0,1:T(8,128)(2,1)}), bf16[32,4,1024]{2,0,1:T(8,128)(2,1)S(1)}, u32[]{:S(2)}, u32[]{:S(2)}) async-start(bf16[32,4,1024]{2,0,1:T(8,128)(2,1)} %bitcast.226), calls=%async_computation.2 | async-start | bytes 524288 | tf_op jit(solution)/shard_map/all_to_all | solution.py:177
  200.7 77.7 %collective-permute-start.1 = (bf16[2,128,8,128]{3,1,2,0:T(8,128)(2,1)S(1)}, bf16[2,128,8,128]{3,1,2,0:T(8,128)(2,1)}, u32[]{:S(2)}, u32[]{:S(2)}) collective-permute-start(bf16[2,128,8,128]{3,1,2,0:T(8,128)(2,1)S(1)} %pad_maximum_fusion), channel_id=1, source_target_pairs={{0,4},{4,8},{8,12},{12,16},{16,20},{20,24},{24,28},{28,32},{32,36}... | collective-permute-start | bytes 1572872 | tf_op jit(solution)/shard_map/while/body/eval_jaxpr/ppermute | solution.py:18
  203.2 12.8 %collective-permute-start = (bf16[2,32,8,128]{3,1,2,0:T(8,128)(2,1)S(1)}, bf16[2,32,8,128]{3,1,2,0:T(8,128)(2,1)S(1)}, u32[]{:S(2)}, u32[]{:S(2)}) collective-permute-start(bf16[2,32,8,128]{3,1,2,0:T(8,128)(2,1)S(1)} %get-tuple-element.334), channel_id=1, source_target_pairs={{0,4},{4,8},{8,12},{12,16},{16,20},{20,24},{24,28},{28,32},{32,36}... | collective-permute-start | bytes 393224 | tf_op jit(solution)/shard_map/while/body/eval_jaxpr/ppermute | solution.py:18
  216.5 9.6 %collective-permute-start = (bf16[2,32,8,128]{3,1,2,0:T(8,128)(2,1)S(1)}, bf16[2,32,8,128]{3,1,2,0:T(8,128)(2,1)S(1)}, u32[]{:S(2)}, u32[]{:S(2)}) collective-permute-start(bf16[2,32,8,128]{3,1,2,0:T(8,128)(2,1)S(1)} %get-tuple-element.334), channel_id=1, source_target_pairs={{0,4},{4,8},{8,12},{12,16},{16,20},{20,24},{24,28},{28,32},{32,36}... | collective-permute-start | bytes 393224 | tf_op jit(solution)/shard_map/while/body/eval_jaxpr/ppermute | solution.py:18
  226.7 9.6 %collective-permute-start = (bf16[2,32,8,128]{3,1,2,0:T(8,128)(2,1)S(1)}, bf16[2,32,8,128]{3,1,2,0:T(8,128)(2,1)S(1)}, u32[]{:S(2)}, u32[]{:S(2)}) collective-permute-start(bf16[2,32,8,128]{3,1,2,0:T(8,128)(2,1)S(1)} %get-tuple-element.334), channel_id=1, source_target_pairs={{0,4},{4,8},{8,12},{12,16},{16,20},{20,24},{24,28},{28,32},{32,36}... | collective-permute-start | bytes 393224 | tf_op jit(solution)/shard_map/while/body/eval_jaxpr/ppermute | solution.py:18
  236.8 9.6 %collective-permute-start = (bf16[2,32,8,128]{3,1,2,0:T(8,128)(2,1)S(1)}, bf16[2,32,8,128]{3,1,2,0:T(8,128)(2,1)S(1)}, u32[]{:S(2)}, u32[]{:S(2)}) collective-permute-start(bf16[2,32,8,128]{3,1,2,0:T(8,128)(2,1)S(1)} %get-tuple-element.334), channel_id=1, source_target_pairs={{0,4},{4,8},{8,12},{12,16},{16,20},{20,24},{24,28},{28,32},{32,36}... | collective-permute-start | bytes 393224 | tf_op jit(solution)/shard_map/while/body/eval_jaxpr/ppermute | solution.py:18
  246.9 9.6 %collective-permute-start = (bf16[2,32,8,128]{3,1,2,0:T(8,128)(2,1)S(1)}, bf16[2,32,8,128]{3,1,2,0:T(8,128)(2,1)S(1)}, u32[]{:S(2)}, u32[]{:S(2)}) collective-permute-start(bf16[2,32,8,128]{3,1,2,0:T(8,128)(2,1)S(1)} %get-tuple-element.334), channel_id=1, source_target_pairs={{0,4},{4,8},{8,12},{12,16},{16,20},{20,24},{24,28},{28,32},{32,36}... | collective-permute-start | bytes 393224 | tf_op jit(solution)/shard_map/while/body/eval_jaxpr/ppermute | solution.py:18
  257.1 9.6 %collective-permute-start = (bf16[2,32,8,128]{3,1,2,0:T(8,128)(2,1)S(1)}, bf16[2,32,8,128]{3,1,2,0:T(8,128)(2,1)S(1)}, u32[]{:S(2)}, u32[]{:S(2)}) collective-permute-start(bf16[2,32,8,128]{3,1,2,0:T(8,128)(2,1)S(1)} %get-tuple-element.334), channel_id=1, source_target_pairs={{0,4},{4,8},{8,12},{12,16},{16,20},{20,24},{24,28},{28,32},{32,36}... | collective-permute-start | bytes 393224 | tf_op jit(solution)/shard_map/while/body/eval_jaxpr/ppermute | solution.py:18
  267.2 9.6 %collective-permute-start = (bf16[2,32,8,128]{3,1,2,0:T(8,128)(2,1)S(1)}, bf16[2,32,8,128]{3,1,2,0:T(8,128)(2,1)S(1)}, u32[]{:S(2)}, u32[]{:S(2)}) collective-permute-start(bf16[2,32,8,128]{3,1,2,0:T(8,128)(2,1)S(1)} %get-tuple-element.334), channel_id=1, source_target_pairs={{0,4},{4,8},{8,12},{12,16},{16,20},{20,24},{24,28},{28,32},{32,36}... | collective-permute-start | bytes 393224 | tf_op jit(solution)/shard_map/while/body/eval_jaxpr/ppermute | solution.py:18
where the time goes:
time: 296 us; the launch traced here: 295 us
  blocking collectives  175 us (59%)
  waiting for transfers between devices  68 us (23%)
  starting transfers between devices  27.7 us (9%)
  matrix products  10.9 us (4%)
  local copies, waits for them, and re-layouts  8.66 us (3%)
  other arithmetic  4 us (1%)
    all_gather x1, blocking collectives, on_device(): lax.all_gather(far_k, 'ctx', axis=0, tiled=True)  85.1 us
    all_gather x1, blocking collectives, on_device(): lax.all_gather(far_v, 'ctx', axis=0, tiled=True)  80.7 us
    ppermute x8, waiting for transfers between devices, shifted(): return lax.ppermute(block, axis, route)  53 us
    ppermute x8, starting transfers between devices, shifted(): return lax.ppermute(block, axis, route)  16.6 us
    all_to_all x1, blocking collectives, on_device(): lax.all_to_all(merged, 'head', split_axis=0, concat_axis=1, tiled=True)  9.07 us
    all_to_all x1, waiting for transfers between devices, on_device(): lax.all_to_all(key_rows, 'head', split_axis=1, concat_axis=0, tiled=True)  6.57 us
    all_to_all x1, waiting for transfers between devices, on_device(): lax.all_to_all(value_rows, 'head', split_axis=1, concat_axis=0, tiled=True)  6.48 us
  transfers between devices with their start and end apart: 11, of which 10 were waited for; matrix products, arithmetic and copies ran while one was open for 4% of the time, Pallas kernels for 0%

commit v1 on v0

v1 whole, which is shorter than its diff:
```python
import math

import jax
import jax.numpy as jnp
from jax import lax
from jax.experimental import pallas as pl
from jax.experimental.pallas import tpu as pltpu
from jax.sharding import Mesh, PartitionSpec as P

DH = 128
BUCKETS = 32
MAXDIST = 128
R1 = 4
R2 = 64
SPAN = 256
PLANES = 16
GROUPS = 8
LANES = 4
PEERS = GROUPS * LANES
ROWS = 32
SEG = PEERS * ROWS
KEPT = SEG // R2
NEG = -1e30
SCALE = DH ** (-0.5)

VMEM = pl.BlockSpec(memory_space=pltpu.VMEM)
SMEM = pl.BlockSpec(memory_space=pltpu.SMEM)


def params():
    return pltpu.CompilerParams(vmem_limit_bytes=24 * 1024 * 1024)


def bucket_starts():
    half = BUCKETS // 2
    starts = list(range(half + 1))
    for target in range(half + 1, BUCKETS):
        starts.append(int(math.ceil(half * (MAXDIST / half) ** ((target - half) / half))))
    return starts


def pack_kernel(q_ref, k_ref, v_ref, out_ref):
    for g in range(GROUPS):
        for x in range(LANES):
            s, h = g * LANES + x, GROUPS * x + g
            cols = slice(h * DH, (h + 1) * DH)
            out_ref[s, 0:ROWS] = q_ref[:, cols]
            out_ref[s, ROWS : 2 * ROWS] = k_ref[:, cols]
            out_ref[s, 2 * ROWS : 3 * ROWS] = v_ref[:, cols]


def unpack_kernel(in_ref, out_ref):
    for g in range(GROUPS):
        for x in range(LANES):
            s, h = g * LANES + x, GROUPS * x + g
            out_ref[:, h * DH : (h + 1) * DH] = in_ref[s]


def bias_kernel(table_ref, where_ref, near_ref, mid_ref, far_ref):
    starts = bucket_starts()
    width = 2 * SPAN
    lane = lax.broadcasted_iota(jnp.int32, (8, width), 1)
    steps = jnp.where(lane == 0, 0, width - lane)

    def line(stride):
        distance = steps * stride
        value = jnp.full((8, width), table_ref[0, 0], jnp.float32)
        for n in range(1, BUCKETS):
            value = jnp.where(distance >= starts[n], table_ref[n, 0], value)
        return jnp.where((lane == 0) | (lane > SPAN), value, NEG)

    def spread(row, count):
        wide = jnp.broadcast_to(row[0:1], (count, width))
        return pltpu.roll(wide, 0, 1, stride=1, stride_axis=0)[:, :SPAN]

    near_ref[...] = spread(line(1), SPAN)
    mid_ref[...] = spread(line(R1), SPAN)
    far_ref[...] = spread(pltpu.roll(line(R2), where_ref[2] * KEPT, 1), KEPT)


def kept_tile(ref, part, pick):
    half = pick // ROWS
    within = pick % ROWS
    tile = (within // 16) * 16
    rows = ref[:, half, pl.ds(pl.multiple_of(part * ROWS + tile, 16), 16), :].astype(jnp.float32)
    spot = lax.broadcasted_iota(jnp.int32, (KEPT, 16, DH), 1)
    return jnp.sum(jnp.where(spot == within - tile, rows, 0.0), axis=1)


def kept_kernel(where_ref, qkv_ref, out_ref):
    pick = where_ref[1]
    keys = kept_tile(qkv_ref, 1, pick).astype(jnp.bfloat16)
    values = kept_tile(qkv_ref, 2, pick).astype(jnp.bfloat16)
    for z in range(PLANES):
        out_ref[z, 0:KEPT] = keys
        out_ref[z, KEPT : 2 * KEPT] = values


def branch(q, k, v, bias):
    scores = lax.dot_general(
        q, k, (((1,), (1,)), ((), ())), preferred_element_type=jnp.float32
    ) * SCALE + bias
    top = jnp.max(scores, axis=1, keepdims=True)
    weight = jnp.exp(scores - top)
    total = jnp.sum(weight, axis=1, keepdims=True)
    acc = jnp.dot(weight.astype(jnp.bfloat16), v, preferred_element_type=jnp.float32)
    shape = acc.shape
    return acc, jnp.broadcast_to(top, shape), jnp.broadcast_to(total, shape)


def merge(one, two):
    acc1, top1, total1 = one
    acc2, top2, total2 = two
    top = jnp.maximum(top1, top2)
    w1, w2 = jnp.exp(top1 - top), jnp.exp(top2 - top)
    return acc1 * w1 + acc2 * w2, top, total1 * w1 + total2 * w2


def local_kernel(
    where_ref, qkv_ref, near_ref, mid_ref, out_ref, far_ref, wide, acc_ref, top_ref, total_ref
):
    near_bias = near_ref[...]
    count = SPAN // ROWS
    for s in range(SEG // SPAN):
        blocks = slice(s * count, (s + 1) * count)
        rows = slice(s * SPAN, (s + 1) * SPAN)
        q = qkv_ref[blocks, 0:ROWS].reshape(SPAN, DH)
        k = qkv_ref[blocks, ROWS : 2 * ROWS].reshape(SPAN, DH)
        v = qkv_ref[blocks, 2 * ROWS : 3 * ROWS].reshape(SPAN, DH)
        wide[0, rows] = q.astype(jnp.float32)
        wide[1, rows] = k.astype(jnp.float32)
        wide[2, rows] = v.astype(jnp.float32)
        acc_ref[rows], top_ref[rows], total_ref[rows] = branch(q, k, v, near_bias)
    kept = pl.ds(where_ref[0], SPAN, stride=R1)
    q, k, v = (wide[n, kept, :].astype(jnp.bfloat16) for n in range(3))
    mid = branch(q, k, v, mid_ref[...])
    merged = merge((acc_ref[kept, :], top_ref[kept, :], total_ref[kept, :]), mid)
    acc_ref[kept, :], top_ref[kept, :], total_ref[kept, :] = merged
    out_ref[...] = (acc_ref[...] / total_ref[...]).astype(jnp.bfloat16).reshape(PEERS, ROWS, DH)
    far = pl.ds(where_ref[1], KEPT, stride=R2)
    far_ref[0] = acc_ref[far, :]
    far_ref[1] = top_ref[far, :]
    far_ref[2] = total_ref[far, :]
    far_ref[3] = wide[0, far, :]


def far_kernel(where_ref, kv_ref, bias_ref, far_ref, in_ref, out_ref):
    q = far_ref[3].astype(jnp.bfloat16)
    k = kv_ref[:, 0:KEPT].reshape(SPAN, DH)
    v = kv_ref[:, KEPT : 2 * KEPT].reshape(SPAN, DH)
    far = branch(q, k, v, bias_ref[...])
    acc, _, total = merge((far_ref[0], far_ref[1], far_ref[2]), far)
    row = (acc / total).astype(jnp.bfloat16).astype(jnp.float32)
    out_ref[...] = in_ref[...]
    pick = where_ref[1]
    half = pick // ROWS
    within = pick % ROWS
    tile = (within // 16) * 16
    spot = lax.broadcasted_iota(jnp.int32, (KEPT, 16, DH), 1)
    rows = pl.ds(pl.multiple_of(tile, 16), 16)
    old = in_ref[:, half, rows, :].astype(jnp.float32)
    new = jnp.where(spot == within - tile, jnp.broadcast_to(row[:, None], old.shape), old)
    out_ref[:, half, rows, :] = new.astype(jnp.bfloat16)


def on_device(queries, key_rows, value_rows, rel_bias, offsets):
    bf16, f32 = jnp.bfloat16, jnp.float32
    group = lax.axis_index("g")
    table = lax.dynamic_slice_in_dim(rel_bias, group, 1, axis=1)
    picks = lax.dynamic_slice_in_dim(offsets, group, 1, axis=1)[:, 0]
    where = jnp.concatenate([picks, lax.axis_index("z").astype(jnp.int32)[None]])
    packed = pl.pallas_call(
        pack_kernel,
        out_shape=jax.ShapeDtypeStruct((PEERS, 3 * ROWS, DH), bf16),
        in_specs=[VMEM] * 3,
        out_specs=VMEM,
        compiler_params=params(),
        name="pack",
    )(queries, key_rows, value_rows)
    near_bias, mid_bias, far_bias = pl.pallas_call(
        bias_kernel,
        out_shape=(
            jax.ShapeDtypeStruct((SPAN, SPAN), f32),
            jax.ShapeDtypeStruct((SPAN, SPAN), f32),
            jax.ShapeDtypeStruct((KEPT, SPAN), f32),
        ),
        in_specs=[SMEM, SMEM],
        out_specs=(VMEM, VMEM, VMEM),
        compiler_params=params(),
        name="bias",
    )(table, where)
    qkv = lax.all_to_all(packed, ("g", "x"), 0, 0, tiled=True)
    kept = pl.pallas_call(
        kept_kernel,
        out_shape=jax.ShapeDtypeStruct((PLANES, 2 * KEPT, DH), bf16),
        in_specs=[SMEM, VMEM],
        out_specs=VMEM,
        compiler_params=params(),
        name="kept",
    )(where, qkv.reshape(KEPT, 2, 3 * ROWS, DH))
    kept = lax.all_to_all(kept, "z", 0, 0, tiled=True)
    local, far_parts = pl.pallas_call(
        local_kernel,
        out_shape=(
            jax.ShapeDtypeStruct((PEERS, ROWS, DH), bf16),
            jax.ShapeDtypeStruct((4, KEPT, DH), f32),
        ),
        in_specs=[SMEM, VMEM, VMEM, VMEM],
        out_specs=(VMEM, VMEM),
        scratch_shapes=[
            pltpu.VMEM((3, SEG, DH), f32),
            pltpu.VMEM((SEG, DH), f32),
            pltpu.VMEM((SEG, DH), f32),
            pltpu.VMEM((SEG, DH), f32),
        ],
        compiler_params=params(),
        name="local",
    )(where, qkv, near_bias, mid_bias)
    merged = pl.pallas_call(
        far_kernel,
        out_shape=jax.ShapeDtypeStruct((KEPT, 2, ROWS, DH), bf16),
        in_specs=[SMEM, VMEM, VMEM, VMEM, VMEM],
        out_specs=VMEM,
        input_output_aliases={4: 0},
        compiler_params=params(),
        name="far",
    )(where, kept, far_bias, far_parts, local.reshape(KEPT, 2, ROWS, DH))
    back = lax.all_to_all(merged.reshape(PEERS, ROWS, DH), ("g", "x"), 0, 0, tiled=True)
    return pl.pallas_call(
        unpack_kernel,
        out_shape=jax.ShapeDtypeStruct((ROWS, PEERS * DH), bf16),
        in_specs=[VMEM],
        out_specs=VMEM,
        compiler_params=params(),
        name="unpack",
    )(back)


def solution(mesh):
    mesh = Mesh(mesh.devices.reshape(PLANES, GROUPS, LANES), ("z", "g", "x"))
    rows = P(("z", "g", "x"), None)
    return jax.shard_map(
        on_device,
        mesh=mesh,
        in_specs=(rows, rows, rows, P(None, "x"), P(None, "x")),
        out_specs=rows,
        check_vma=False,
    )
```

time: 296 us -> 72.3 us (0.24)
  the two profiles are of different devices: /device:TPU:128 before, /device:TPU:1 now
where the time goes in v1:
time: 72.3 us; the launch traced here: 71.9 us
  starting transfers between devices  23.4 us (32%)
  waiting for transfers between devices  22.1 us (31%)
  blocking collectives  15.9 us (22%)
  Pallas kernels  6.6 us (9%)
  local copies, waits for them, and re-layouts  3.82 us (5%)
    all_to_all x1, blocking collectives, on_device(): lax.all_to_all(merged.reshape(PEERS, ROWS, DH), ('g', 'x'), 0, 0, tiled=T...  15.9 us
    all_to_all x1, starting transfers between devices, on_device(): kept = lax.all_to_all(kept, 'z', 0, 0, tiled=True)  13 us
    all_to_all x1, waiting for transfers between devices, on_device(): qkv = lax.all_to_all(packed, ('g', 'x'), 0, 0, tiled=True)  12.8 us
    all_to_all x1, starting transfers between devices, on_device(): qkv = lax.all_to_all(packed, ('g', 'x'), 0, 0, tiled=True)  10.5 us
    all_to_all x1, waiting for transfers between devices, on_device(): kept = lax.all_to_all(kept, 'z', 0, 0, tiled=True)  9.26 us
    unnamed x11, local copies, waits for them, and re-layouts  3.63 us
    pallas_call x1, Pallas kernels, on_device(): pl.pallas_call(local_kernel, out_shape=(jax.ShapeDtypeStruct((PEERS, ROWS...  1.56 us
  transfers between devices with their start and end apart: 2, of which 2 were waited for; matrix products, arithmetic and copies ran while one was open for 1% of the time, Pallas kernels for 4%

profile of v1, /device:TPU:1, one launch (start us, length us, event | category | flops | bytes accessed | tf_op | source)
XLA Modules:
  0.0 71.9 jit_solution(18235978986417817950)
XLA Ops:
  0.0 0.0 copy-start
  0.0 0.0 copy-start.1
  0.0 1.0 %copy-done.1 = bf16[32,4096]{1,0:T(8,128)(2,1)S(1)} copy-done((bf16[32,4096]{1,0:T(8,128)(2,1)S(1)}, bf16[32,4096]{1,0:T(8,128)(2,1)}, u32[]{:S(2)}) %copy-start.1) | copy-done | bytes 262168
  1.0 0.0 copy-start.2
  1.0 0.9 %copy-done.2 = bf16[32,4096]{1,0:T(8,128)(2,1)S(1)} copy-done((bf16[32,4096]{1,0:T(8,128)(2,1)S(1)}, bf16[32,4096]{1,0:T(8,128)(2,1)}, u32[]{:S(2)}) %copy-start.2) | copy-done | bytes 262168
  1.9 0.0 copy-start.3
  1.9 0.9 %copy-done.3 = bf16[32,4096]{1,0:T(8,128)(2,1)S(1)} copy-done((bf16[32,4096]{1,0:T(8,128)(2,1)S(1)}, bf16[32,4096]{1,0:T(8,128)(2,1)}, u32[]{:S(2)}) %copy-start.3) | copy-done | bytes 262168
  2.9 1.0 %pack.1 = bf16[32,96,128]{2,1,0:T(8,128)(2,1)} custom-call(bf16[32,4096]{1,0:T(8,128)(2,1)S(1)} %copy-done.1, bf16[32,4096]{1,0:T(8,128)(2,1)S(1)} %copy-done.2, bf16[32,4096]{1,0:T(8,128)(2,1)S(1)} %copy-done.3), custom_call_target="tpu_custom_call" | custom-call | tf_op jit(solution)/shard_map/pack/pallas_call | solution.py:172
  3.9 10.5 %all-to-all-start = ((bf16[32,96,128]{2,1,0:T(8,128)(2,1)}), bf16[32,96,128]{2,1,0:T(8,128)(2,1)S(1)}, u32[]{:S(2)}, u32[]{:S(2)}) async-start(bf16[32,96,128]{2,1,0:T(8,128)(2,1)} %pack.1), calls=%async_computation | async-start | bytes 1572864 | tf_op jit(solution)/shard_map/all_to_all | solution.py:192
  14.4 0.0 copy-start.4
  14.4 0.7 copy-done.4
  15.1 0.2 dynamic-slice_reduce_fusion
  15.2 0.1 pad_add_fusion.where_ref
  15.3 12.8 %all-to-all-done.qkv_ref = bf16[32,96,128]{2,1,0:T(8,128)(2,1)S(1)} async-done(((bf16[32,96,128]{2,1,0:T(8,128)(2,1)}), bf16[32,96,128]{2,1,0:T(8,128)(2,1)S(1)}, u32[]{:S(2)}, u32[]{:S(2)}) %all-to-all-start) | async-done | bytes 786464 | tf_op jit(solution)/shard_map/all_to_all | solution.py:192
  28.1 1.3 %kept.1 = bf16[16,32,128]{2,1,0:T(8,128)(2,1)} custom-call(s32[3]{0:T(128)S(1)} %pad_add_fusion.where_ref, bf16[16,2,96,128]{3,2,1,0:T(8,128)(2,1)S(1)} %bitcast.4), custom_call_target="tpu_custom_call" | custom-call | tf_op jit(solution)/shard_map/kept/pallas_call | solution.py:193
  29.4 13.0 %all-to-all-start.1 = ((bf16[16,32,128]{2,1,0:T(8,128)(2,1)}), bf16[16,32,128]{2,1,0:T(8,128)(2,1)S(1)}, u32[]{:S(2)}, u32[]{:S(2)}) async-start(bf16[16,32,128]{2,1,0:T(8,128)(2,1)} %kept.1), calls=%async_computation.1 | async-start | bytes 262144 | tf_op jit(solution)/shard_map/all_to_all | solution.py:201
  42.4 0.0 copy-done
  42.4 0.1 copy.8.table_ref
  42.5 1.0 %bias.1 = (f32[256,256]{1,0:T(8,128)S(1)}, f32[256,256]{1,0:T(8,128)S(1)}, f32[16,256]{1,0:T(8,128)S(1)}) custom-call(f32[32,1]{1,0:T(8,128)S(1)} %copy.8.table_ref, s32[3]{0:T(128)S(1)} %pad_add_fusion.where_ref), custom_call_target="tpu_custom_call" | custom-call | tf_op jit(solution)/shard_map/bias/pallas_call | solution.py:180
  43.5 1.6 %local.1 = (bf16[32,32,128]{2,1,0:T(8,128)(2,1)S(1)}, f32[4,16,128]{2,1,0:T(8,128)S(1)}) custom-call(s32[3]{0:T(128)S(1)} %pad_add_fusion.where_ref, bf16[32,96,128]{2,1,0:T(8,128)(2,1)S(1)} %all-to-all-done.qkv_ref, f32[256,256]{1,0:T(8,128)S(1)} %get-tuple-element.11.near_ref, f32[256,256]{1,0:T(8,128)S(1)} %get-tuple-element.12.mid_ref), custom_call_target="tpu_custom_call" | custom-call | tf_op jit(solution)/shard_map/local/pallas_call | solution.py:202
  45.1 9.3 %all-to-all-done.1.kv_ref = bf16[16,32,128]{2,1,0:T(8,128)(2,1)S(1)} async-done(((bf16[16,32,128]{2,1,0:T(8,128)(2,1)}), bf16[16,32,128]{2,1,0:T(8,128)(2,1)S(1)}, u32[]{:S(2)}, u32[]{:S(2)}) %all-to-all-start.1) | async-done | bytes 131104 | tf_op jit(solution)/shard_map/all_to_all | solution.py:201
  54.4 0.9 %far.1 = bf16[16,2,32,128]{3,2,1,0:T(8,128)(2,1)S(1)} custom-call(s32[3]{0:T(128)S(1)} %pad_add_fusion.where_ref, bf16[16,32,128]{2,1,0:T(8,128)(2,1)S(1)} %all-to-all-done.1.kv_ref, f32[16,256]{1,0:T(8,128)S(1)} %get-tuple-element.10.bias_ref, f32[4,16,128]{2,1,0:T(8,128)S(1)} %get-tuple-element.13.far_ref, ...), custom_call_target="tpu_custom_call", output_to_operand_aliasing={{}: (4, {})} | custom-call | tf_op jit(solution)/shard_map/far/pallas_call | solution.py:219
  55.3 15.9 %all_to_all.15.in_ref = bf16[32,32,128]{2,1,0:T(8,128)(2,1)S(1)} all-to-all(bf16[32,32,128]{2,1,0:T(8,128)(2,1)S(1)} %bitcast.6), channel_id=1, replica_groups=mesh['z'=16,'g'=8,'x'=4] {'g','x'}, dimensions={0} | all-to-all | bytes 524288 | tf_op jit(solution)/shard_map/all_to_all | solution.py:228
  71.2 0.8 %unpack.1 = bf16[32,4096]{1,0:T(8,128)(2,1)} custom-call(bf16[32,32,128]{2,1,0:T(8,128)(2,1)S(1)} %all_to_all.15.in_ref), custom_call_target="tpu_custom_call" | custom-call | tf_op jit(solution)/shard_map/unpack/pallas_call | solution.py:229
  (1 shorter events, 0.0 us)
Async XLA Ops:
  0.0 42.4 %copy-start = (f32[32,8]{0,1:T(8,128)S(1)}, f32[32,8]{0,1:T(8,128)}, u32[]{:S(2)}) copy-start(f32[32,8]{0,1:T(8,128)} %param.8) | copy-start | bytes 3076
  0.0 1.0 %copy-start.1 = (bf16[32,4096]{1,0:T(8,128)(2,1)S(1)}, bf16[32,4096]{1,0:T(8,128)(2,1)}, u32[]{:S(2)}) copy-start(bf16[32,4096]{1,0:T(8,128)(2,1)} %q_ref.1) | copy-start | bytes 786436
  1.0 0.9 %copy-start.2 = (bf16[32,4096]{1,0:T(8,128)(2,1)S(1)}, bf16[32,4096]{1,0:T(8,128)(2,1)}, u32[]{:S(2)}) copy-start(bf16[32,4096]{1,0:T(8,128)(2,1)} %k_ref.1) | copy-start | bytes 786436
  1.9 0.9 %copy-start.3 = (bf16[32,4096]{1,0:T(8,128)(2,1)S(1)}, bf16[32,4096]{1,0:T(8,128)(2,1)}, u32[]{:S(2)}) copy-start(bf16[32,4096]{1,0:T(8,128)(2,1)} %v_ref.1) | copy-start | bytes 786436
  3.9 24.2 %all-to-all-start = ((bf16[32,96,128]{2,1,0:T(8,128)(2,1)}), bf16[32,96,128]{2,1,0:T(8,128)(2,1)S(1)}, u32[]{:S(2)}, u32[]{:S(2)}) async-start(bf16[32,96,128]{2,1,0:T(8,128)(2,1)} %pack.1), calls=%async_computation | async-start | bytes 1572864 | tf_op jit(solution)/shard_map/all_to_all | solution.py:192
  14.4 0.7 copy-start.4
  29.4 25.0 %all-to-all-start.1 = ((bf16[16,32,128]{2,1,0:T(8,128)(2,1)}), bf16[16,32,128]{2,1,0:T(8,128)(2,1)S(1)}, u32[]{:S(2)}, u32[]{:S(2)}) async-start(bf16[16,32,128]{2,1,0:T(8,128)(2,1)} %kept.1), calls=%async_computation.1 | async-start | bytes 262144 | tf_op jit(solution)/shard_map/all_to_all | solution.py:201

commit v2 on v1

--- a/solution.py
+++ b/solution.py
@@ -25,6 +25,7 @@
 
 VMEM = pl.BlockSpec(memory_space=pltpu.VMEM)
 SMEM = pl.BlockSpec(memory_space=pltpu.SMEM)
+HBM = pl.BlockSpec(memory_space=pltpu.HBM)
 
 
 def params():
@@ -39,14 +40,30 @@
     return starts
 
 
-def pack_kernel(q_ref, k_ref, v_ref, out_ref):
-    for g in range(GROUPS):
-        for x in range(LANES):
-            s, h = g * LANES + x, GROUPS * x + g
-            cols = slice(h * DH, (h + 1) * DH)
-            out_ref[s, 0:ROWS] = q_ref[:, cols]
-            out_ref[s, ROWS : 2 * ROWS] = k_ref[:, cols]
-            out_ref[s, 2 * ROWS : 3 * ROWS] = v_ref[:, cols]
+def pack_kernel(q_ref, k_ref, v_ref, offsets_ref, out_ref, picks_ref, sems):
+    copies = [pltpu.make_async_copy(offsets_ref, picks_ref, sems.at[3])]
+    for n, ref in enumerate((q_ref, k_ref, v_ref)):
+        for g in range(GROUPS):
+            for x in range(LANES):
+                s, h = g * LANES + x, GROUPS * x + g
+                copies.append(
+                    pltpu.make_async_copy(
+                        ref.at[:, h * DH : (h + 1) * DH],
+                        out_ref.at[s, n * ROWS : (n + 1) * ROWS],
+                        sems.at[n],
+                    )
+                )
+    for copy in copies:
+        copy.start()
+    for copy in copies:
+        copy.wait()
+
+
+def offset_of(ref, row):
+    values = ref[...]
+    at_row = lax.broadcasted_iota(jnp.int32, values.shape, 0) == row
+    at_head = lax.broadcasted_iota(jnp.int32, values.shape, 1) == lax.axis_index("g")
+    return jnp.sum(jnp.where(at_row & at_head, values, 0))
 
 
 def unpack_kernel(in_ref, out_ref):
@@ -56,17 +73,18 @@
             out_ref[:, h * DH : (h + 1) * DH] = in_ref[s]
 
 
-def bias_kernel(table_ref, where_ref, near_ref, mid_ref, far_ref):
+def bias_kernel(table_ref, near_ref, mid_ref, far_ref):
     starts = bucket_starts()
+    head = lax.axis_index("g")
     width = 2 * SPAN
     lane = lax.broadcasted_iota(jnp.int32, (8, width), 1)
     steps = jnp.where(lane == 0, 0, width - lane)
 
     def line(stride):
         distance = steps * stride
-        value = jnp.full((8, width), table_ref[0, 0], jnp.float32)
+        value = jnp.full((8, width), table_ref[0, head], jnp.float32)
         for n in range(1, BUCKETS):
-            value = jnp.where(distance >= starts[n], table_ref[n, 0], value)
+            value = jnp.where(distance >= starts[n], table_ref[n, head], value)
         return jnp.where((lane == 0) | (lane > SPAN), value, NEG)
 
     def spread(row, count):
@@ -75,7 +93,7 @@
 
     near_ref[...] = spread(line(1), SPAN)
     mid_ref[...] = spread(line(R1), SPAN)
-    far_ref[...] = spread(pltpu.roll(line(R2), where_ref[2] * KEPT, 1), KEPT)
+    far_ref[...] = spread(pltpu.roll(line(R2), lax.axis_index("z") * KEPT, 1), KEPT)
 
 
 def kept_tile(ref, part, pick):
@@ -87,8 +105,8 @@
     return jnp.sum(jnp.where(spot == within - tile, rows, 0.0), axis=1)
 
 
-def kept_kernel(where_ref, qkv_ref, out_ref):
-    pick = where_ref[1]
+def kept_kernel(offsets_ref, qkv_ref, out_ref):
+    pick = offset_of(offsets_ref, 1)
     keys = kept_tile(qkv_ref, 1, pick).astype(jnp.bfloat16)
     values = kept_tile(qkv_ref, 2, pick).astype(jnp.bfloat16)
     for z in range(PLANES):
@@ -117,7 +135,7 @@
 
 
 def local_kernel(
-    where_ref, qkv_ref, near_ref, mid_ref, out_ref, far_ref, wide, acc_ref, top_ref, total_ref
+    offsets_ref, qkv_ref, near_ref, mid_ref, out_ref, far_ref, wide, acc_ref, top_ref, total_ref
 ):
     near_bias = near_ref[...]
     count = SPAN // ROWS
@@ -131,20 +149,20 @@
         wide[1, rows] = k.astype(jnp.float32)
         wide[2, rows] = v.astype(jnp.float32)
         acc_ref[rows], top_ref[rows], total_ref[rows] = branch(q, k, v, near_bias)
-    kept = pl.ds(where_ref[0], SPAN, stride=R1)
+    kept = pl.ds(offset_of(offsets_ref, 0), SPAN, stride=R1)
     q, k, v = (wide[n, kept, :].astype(jnp.bfloat16) for n in range(3))
     mid = branch(q, k, v, mid_ref[...])
     merged = merge((acc_ref[kept, :], top_ref[kept, :], total_ref[kept, :]), mid)
     acc_ref[kept, :], top_ref[kept, :], total_ref[kept, :] = merged
     out_ref[...] = (acc_ref[...] / total_ref[...]).astype(jnp.bfloat16).reshape(PEERS, ROWS, DH)
-    far = pl.ds(where_ref[1], KEPT, stride=R2)
+    far = pl.ds(offset_of(offsets_ref, 1), KEPT, stride=R2)
     far_ref[0] = acc_ref[far, :]
     far_ref[1] = top_ref[far, :]
     far_ref[2] = total_ref[far, :]
     far_ref[3] = wide[0, far, :]
 
 
-def far_kernel(where_ref, kv_ref, bias_ref, far_ref, in_ref, out_ref):
+def far_kernel(offsets_ref, kv_ref, bias_ref, far_ref, in_ref, out_ref):
     q = far_ref[3].astype(jnp.bfloat16)
     k = kv_ref[:, 0:KEPT].reshape(SPAN, DH)
     v = kv_ref[:, KEPT : 2 * KEPT].reshape(SPAN, DH)
@@ -152,7 +170,7 @@
     acc, _, total = merge((far_ref[0], far_ref[1], far_ref[2]), far)
     row = (acc / total).astype(jnp.bfloat16).astype(jnp.float32)
     out_ref[...] = in_ref[...]
-    pick = where_ref[1]
+    pick = offset_of(offsets_ref, 1)
     half = pick // ROWS
     within = pick % ROWS
     tile = (within // 16) * 16
@@ -165,18 +183,29 @@
 
 def on_device(queries, key_rows, value_rows, rel_bias, offsets):
     bf16, f32 = jnp.bfloat16, jnp.float32
-    group = lax.axis_index("g")
-    table = lax.dynamic_slice_in_dim(rel_bias, group, 1, axis=1)
-    picks = lax.dynamic_slice_in_dim(offsets, group, 1, axis=1)[:, 0]
-    where = jnp.concatenate([picks, lax.axis_index("z").astype(jnp.int32)[None]])
-    packed = pl.pallas_call(
+    given = (queries, key_rows, value_rows, offsets)
+    packed, picks = pl.pallas_call(
         pack_kernel,
-        out_shape=jax.ShapeDtypeStruct((PEERS, 3 * ROWS, DH), bf16),
-        in_specs=[VMEM] * 3,
+        out_shape=(
+            jax.ShapeDtypeStruct((PEERS, 3 * ROWS, DH), bf16),
+            jax.ShapeDtypeStruct(offsets.shape, offsets.dtype),
+        ),
+        in_specs=[HBM] * 4,
+        out_specs=(VMEM, VMEM),
+        scratch_shapes=[pltpu.SemaphoreType.DMA((4,))],
+        compiler_params=params(),
+        name="pack",
+    )(*(pltpu.with_memory_space_constraint(t, pltpu.HBM) for t in given))
+    qkv = lax.all_to_all(packed, ("g", "x"), 0, 0, tiled=True)
+    kept = pl.pallas_call(
+        kept_kernel,
+        out_shape=jax.ShapeDtypeStruct((PLANES, 2 * KEPT, DH), bf16),
+        in_specs=[VMEM, VMEM],
         out_specs=VMEM,
         compiler_params=params(),
-        name="pack",
-    )(queries, key_rows, value_rows)
+        name="kept",
+    )(picks, qkv.reshape(KEPT, 2, 3 * ROWS, DH))
+    kept = lax.all_to_all(kept, "z", 0, 0, tiled=True)
     near_bias, mid_bias, far_bias = pl.pallas_call(
         bias_kernel,
         out_shape=(
@@ -184,28 +213,18 @@
             jax.ShapeDtypeStruct((SPAN, SPAN), f32),
             jax.ShapeDtypeStruct((KEPT, SPAN), f32),
         ),
-        in_specs=[SMEM, SMEM],
+        in_specs=[SMEM],
         out_specs=(VMEM, VMEM, VMEM),
         compiler_params=params(),
         name="bias",
-    )(table, where)
-    qkv = lax.all_to_all(packed, ("g", "x"), 0, 0, tiled=True)
-    kept = pl.pallas_call(
-        kept_kernel,
-        out_shape=jax.ShapeDtypeStruct((PLANES, 2 * KEPT, DH), bf16),
-        in_specs=[SMEM, VMEM],
-        out_specs=VMEM,
-        compiler_params=params(),
-        name="kept",
-    )(where, qkv.reshape(KEPT, 2, 3 * ROWS, DH))
-    kept = lax.all_to_all(kept, "z", 0, 0, tiled=True)
+    )(rel_bias)
     local, far_parts = pl.pallas_call(
         local_kernel,
         out_shape=(
             jax.ShapeDtypeStruct((PEERS, ROWS, DH), bf16),
             jax.ShapeDtypeStruct((4, KEPT, DH), f32),
         ),
-        in_specs=[SMEM, VMEM, VMEM, VMEM],
+        in_specs=[VMEM] * 4,
         out_specs=(VMEM, VMEM),
         scratch_shapes=[
             pltpu.VMEM((3, SEG, DH), f32),
@@ -215,16 +234,16 @@
         ],
         compiler_params=params(),
         name="local",
-    )(where, qkv, near_bias, mid_bias)
+    )(picks, qkv, near_bias, mid_bias)
     merged = pl.pallas_call(
         far_kernel,
         out_shape=jax.ShapeDtypeStruct((KEPT, 2, ROWS, DH), bf16),
-        in_specs=[SMEM, VMEM, VMEM, VMEM, VMEM],
+        in_specs=[VMEM] * 5,
         out_specs=VMEM,
         input_output_aliases={4: 0},
         compiler_params=params(),
         name="far",
-    )(where, kept, far_bias, far_parts, local.reshape(KEPT, 2, ROWS, DH))
+    )(picks, kept, far_bias, far_parts, local.reshape(KEPT, 2, ROWS, DH))
     back = lax.all_to_all(merged.reshape(PEERS, ROWS, DH), ("g", "x"), 0, 0, tiled=True)
     return pl.pallas_call(
         unpack_kernel,

time: 72.3 us -> 68.6 us (0.949)
  blocking collectives: 15.9 us -> 39.2 us
  waiting for transfers between devices: 22.1 us -> 9.81 us
  starting transfers between devices: 23.4 us -> 13.8 us
  local copies, waits for them, and re-layouts: 3.82 us -> 0.08 us
  Pallas kernels: 6.6 us -> 5.36 us
    all_to_all x0 -> x1, blocking collectives: none -> 23.3 us  [on_device(): qkv = lax.all_to_all(packed, ('g', 'x'), 0, 0, tiled=True)]
    all_to_all x1 -> x0, waiting for transfers between devices: 12.8 us -> none  [on_device(): qkv = lax.all_to_all(packed, ('g', 'x'), 0, 0, tiled=True)]
    all_to_all x1 -> x0, starting transfers between devices: 10.5 us -> none  [on_device(): qkv = lax.all_to_all(packed, ('g', 'x'), 0, 0, tiled=True)]
    unnamed x11 -> x3, local copies, waits for them, and re-layouts: 3.63 us -> 0.08 us
    all_to_all x1, starting transfers between devices: 13 us -> 13.8 us  [on_device(): kept = lax.all_to_all(kept, 'z', 0, 0, tiled=True)]
  transfers between devices with their start and end apart: 2 -> 1, of which waited for: 2 -> 1; matrix products, arithmetic and copies ran while one was open for 1% -> 0% of each run, Pallas kernels for 4% -> 3%
where the time goes in v2:
time: 68.6 us; the launch traced here: 68.3 us
  blocking collectives  39.2 us (57%)
  starting transfers between devices  13.8 us (20%)
  waiting for transfers between devices  9.81 us (14%)
  Pallas kernels  5.36 us (8%)
    all_to_all x1, blocking collectives, on_device(): qkv = lax.all_to_all(packed, ('g', 'x'), 0, 0, tiled=True)  23.3 us
    all_to_all x1, blocking collectives, on_device(): lax.all_to_all(merged.reshape(PEERS, ROWS, DH), ('g', 'x'), 0, 0, tiled=T...  15.9 us
    all_to_all x1, starting transfers between devices, on_device(): kept = lax.all_to_all(kept, 'z', 0, 0, tiled=True)  13.8 us
    all_to_all x1, waiting for transfers between devices, on_device(): kept = lax.all_to_all(kept, 'z', 0, 0, tiled=True)  9.81 us
  transfers between devices with their start and end apart: 1, of which 1 were waited for; matrix products, arithmetic and copies ran while one was open for 0% of the time, Pallas kernels for 3%

profile of v2, /device:TPU:1, one launch (start us, length us, event | category | flops | bytes accessed | tf_op | source)
XLA Modules:
  0.0 68.3 jit_solution(8784714625154600812)
XLA Ops:
  0.0 1.2 %pack.1 = (bf16[32,96,128]{2,1,0:T(8,128)(2,1)S(1)}, s32[2,8]{1,0:T(2,128)S(1)}) custom-call(bf16[32,4096]{1,0:T(8,128)(2,1)} %q_ref.1, bf16[32,4096]{1,0:T(8,128)(2,1)} %k_ref.1, bf16[32,4096]{1,0:T(8,128)(2,1)} %v_ref.1, s32[2,8]{1,0:T(2,128)} %offsets_ref.1), custom_call_target="tpu_custom_call" | custom-call | tf_op jit(solution)/shard_map/pack/pallas_call | solution.py:187
  1.3 23.3 %all_to_all.15.qkv_ref = bf16[32,96,128]{2,1,0:T(8,128)(2,1)S(1)} all-to-all(bf16[32,96,128]{2,1,0:T(8,128)(2,1)S(1)} %get-tuple-element.13), channel_id=1, replica_groups=mesh['z'=16,'g'=8,'x'=4] {'g','x'}, dimensions={0} | all-to-all | bytes 1572864 | tf_op jit(solution)/shard_map/all_to_all | solution.py:199
  24.6 0.9 %kept.1 = bf16[16,32,128]{2,1,0:T(8,128)(2,1)} custom-call(s32[2,8]{1,0:T(2,128)S(1)} %get-tuple-element.12.offsets_ref, bf16[16,2,96,128]{3,2,1,0:T(8,128)(2,1)S(1)} %bitcast.3), custom_call_target="tpu_custom_call" | custom-call | tf_op jit(solution)/shard_map/kept/pallas_call | solution.py:200
  25.4 0.0 copy-start
  25.4 13.8 %all-to-all-start.1 = ((bf16[16,32,128]{2,1,0:T(8,128)(2,1)}), bf16[16,32,128]{2,1,0:T(8,128)(2,1)S(1)}, u32[]{:S(2)}, u32[]{:S(2)}) async-start(bf16[16,32,128]{2,1,0:T(8,128)(2,1)} %kept.1), calls=%async_computation.1 | async-start | bytes 262144 | tf_op jit(solution)/shard_map/all_to_all | solution.py:208
  39.2 0.0 copy-done
  39.3 0.1 copy.7.table_ref
  39.3 1.1 %bias.1 = (f32[256,256]{1,0:T(8,128)S(1)}, f32[256,256]{1,0:T(8,128)S(1)}, f32[16,256]{1,0:T(8,128)S(1)}) custom-call(f32[32,8]{1,0:T(8,128)S(1)} %copy.7.table_ref), custom_call_target="tpu_custom_call" | custom-call | tf_op jit(solution)/shard_map/bias/pallas_call | solution.py:209
  40.4 1.0 %local.1 = (bf16[32,32,128]{2,1,0:T(8,128)(2,1)S(1)}, f32[4,16,128]{2,1,0:T(8,128)S(1)}) custom-call(s32[2,8]{1,0:T(2,128)S(1)} %get-tuple-element.12.offsets_ref, bf16[32,96,128]{2,1,0:T(8,128)(2,1)S(1)} %all_to_all.15.qkv_ref, f32[256,256]{1,0:T(8,128)S(1)} %get-tuple-element.15.near_ref, f32[256,256]{1,0:T(8,128)S(1)} %get-tuple-element.16.mid_ref), custom_call_target="tpu_custom_call" | custom-call | tf_op jit(solution)/shard_map/local/pallas_call | solution.py:221
  41.4 9.8 %all-to-all-done.1.kv_ref = bf16[16,32,128]{2,1,0:T(8,128)(2,1)S(1)} async-done(((bf16[16,32,128]{2,1,0:T(8,128)(2,1)}), bf16[16,32,128]{2,1,0:T(8,128)(2,1)S(1)}, u32[]{:S(2)}, u32[]{:S(2)}) %all-to-all-start.1) | async-done | bytes 131104 | tf_op jit(solution)/shard_map/all_to_all | solution.py:208
  51.2 0.4 far.1
  51.6 15.9 %all_to_all.16.in_ref = bf16[32,32,128]{2,1,0:T(8,128)(2,1)S(1)} all-to-all(bf16[32,32,128]{2,1,0:T(8,128)(2,1)S(1)} %bitcast.5), channel_id=1, replica_groups=mesh['z'=16,'g'=8,'x'=4] {'g','x'}, dimensions={0} | all-to-all | bytes 524288 | tf_op jit(solution)/shard_map/all_to_all | solution.py:247
  67.5 0.8 %unpack.1 = bf16[32,4096]{1,0:T(8,128)(2,1)} custom-call(bf16[32,32,128]{2,1,0:T(8,128)(2,1)S(1)} %all_to_all.16.in_ref), custom_call_target="tpu_custom_call" | custom-call | tf_op jit(solution)/shard_map/unpack/pallas_call | solution.py:248
Async XLA Ops:
  25.4 13.8 %copy-start = (f32[32,8]{0,1:T(8,128)S(1)}, f32[32,8]{0,1:T(8,128)}, u32[]{:S(2)}) copy-start(f32[32,8]{0,1:T(8,128)} %param.8) | copy-start | bytes 3076
  25.4 25.8 %all-to-all-start.1 = ((bf16[16,32,128]{2,1,0:T(8,128)(2,1)}), bf16[16,32,128]{2,1,0:T(8,128)(2,1)S(1)}, u32[]{:S(2)}, u32[]{:S(2)}) async-start(bf16[16,32,128]{2,1,0:T(8,128)(2,1)} %kept.1), calls=%async_computation.1 | async-start | bytes 262144 | tf_op jit(solution)/shard_map/all_to_all | solution.py:208

commit v3 on v2

--- a/solution.py
+++ b/solution.py
@@ -20,6 +20,12 @@
 ROWS = 32
 SEG = PEERS * ROWS
 KEPT = SEG // R2
+RING = [8, 0, 1, 15, 2, 14, 3, 13, 4, 12, 5, 11, 6, 10, 7, 9]
+ORDER_IN = [(2 * y + c) * LANES + x for c in (0, 1) for y in (3, 2, 1, 0) for x in (3, 2, 1, 0)]
+ORDER_OUT = [(2 * y + c) * LANES + x for c in (0, 1) for y in (0, 1, 2, 3) for x in (0, 1, 2, 3)]
+PAIRS_IN = [n // 2 for n in ORDER_IN[::2]]
+PAIRS_OUT = [n // 2 for n in ORDER_OUT[::2]]
+PLACE = {n: p for p, n in enumerate(ORDER_IN)}
 NEG = -1e30
 SCALE = DH ** (-0.5)
 
@@ -45,11 +51,11 @@
     for n, ref in enumerate((q_ref, k_ref, v_ref)):
         for g in range(GROUPS):
             for x in range(LANES):
-                s, h = g * LANES + x, GROUPS * x + g
+                p, h = PLACE[g * LANES + x], GROUPS * x + g
                 copies.append(
                     pltpu.make_async_copy(
                         ref.at[:, h * DH : (h + 1) * DH],
-                        out_ref.at[s, n * ROWS : (n + 1) * ROWS],
+                        out_ref.at[p, n * ROWS : (n + 1) * ROWS],
                         sems.at[n],
                     )
                 )
@@ -67,10 +73,9 @@
 
 
 def unpack_kernel(in_ref, out_ref):
-    for g in range(GROUPS):
-        for x in range(LANES):
-            s, h = g * LANES + x, GROUPS * x + g
-            out_ref[:, h * DH : (h + 1) * DH] = in_ref[s]
+    for p, n in enumerate(ORDER_OUT):
+        h = GROUPS * (n % LANES) + n // LANES
+        out_ref[:, h * DH : (h + 1) * DH] = in_ref[p]
 
 
 def bias_kernel(table_ref, near_ref, mid_ref, far_ref):
@@ -80,12 +85,14 @@
     lane = lax.broadcasted_iota(jnp.int32, (8, width), 1)
     steps = jnp.where(lane == 0, 0, width - lane)
 
-    def line(stride):
-        distance = steps * stride
-        value = jnp.full((8, width), table_ref[0, head], jnp.float32)
+    def value_at(distance):
+        value = jnp.full(distance.shape, table_ref[0, head], jnp.float32)
         for n in range(1, BUCKETS):
             value = jnp.where(distance >= starts[n], table_ref[n, head], value)
-        return jnp.where((lane == 0) | (lane > SPAN), value, NEG)
+        return value
+
+    def line(stride):
+        return jnp.where((lane == 0) | (lane > SPAN), value_at(steps * stride), NEG)
 
     def spread(row, count):
         wide = jnp.broadcast_to(row[0:1], (count, width))
@@ -93,16 +100,26 @@
 
     near_ref[...] = spread(line(1), SPAN)
     mid_ref[...] = spread(line(R1), SPAN)
-    far_ref[...] = spread(pltpu.roll(line(R2), lax.axis_index("z") * KEPT, 1), KEPT)
+    row = lax.broadcasted_iota(jnp.int32, (KEPT, SPAN), 0)
+    column = lax.broadcasted_iota(jnp.int32, (KEPT, SPAN), 1)
+    plane = jnp.zeros((KEPT, SPAN), jnp.int32)
+    for n in range(PLANES):
+        plane = jnp.where(column // KEPT == n, RING[n], plane)
+    query, key = jnp.zeros((KEPT, SPAN), jnp.int32), jnp.zeros((KEPT, SPAN), jnp.int32)
+    for n in range(KEPT):
+        query = jnp.where(row == n, PAIRS_OUT[n], query)
+        key = jnp.where(column % KEPT == n, PAIRS_IN[n], key)
+    apart = (lax.axis_index("z") - plane) * KEPT + query - key
+    far_ref[...] = jnp.where(apart >= 0, value_at(apart * R2), NEG)
 
 
 def kept_tile(ref, part, pick):
     half = pick // ROWS
     within = pick % ROWS
     tile = (within // 16) * 16
-    rows = ref[:, half, pl.ds(pl.multiple_of(part * ROWS + tile, 16), 16), :].astype(jnp.float32)
+    rows = ref[:, 1 - half, pl.ds(pl.multiple_of(part * ROWS + tile, 16), 16), :]
     spot = lax.broadcasted_iota(jnp.int32, (KEPT, 16, DH), 1)
-    return jnp.sum(jnp.where(spot == within - tile, rows, 0.0), axis=1)
+    return jnp.sum(jnp.where(spot == within - tile, rows.astype(jnp.float32), 0.0), axis=1)
 
 
 def kept_kernel(offsets_ref, qkv_ref, out_ref):
@@ -140,11 +157,12 @@
     near_bias = near_ref[...]
     count = SPAN // ROWS
     for s in range(SEG // SPAN):
-        blocks = slice(s * count, (s + 1) * count)
+        blocks = [PLACE[n] for n in range(s * count, (s + 1) * count)]
         rows = slice(s * SPAN, (s + 1) * SPAN)
-        q = qkv_ref[blocks, 0:ROWS].reshape(SPAN, DH)
-        k = qkv_ref[blocks, ROWS : 2 * ROWS].reshape(SPAN, DH)
-        v = qkv_ref[blocks, 2 * ROWS : 3 * ROWS].reshape(SPAN, DH)
+        q, k, v = (
+            jnp.concatenate([qkv_ref[p, n * ROWS : (n + 1) * ROWS] for p in blocks], axis=0)
+            for n in range(3)
+        )
         wide[0, rows] = q.astype(jnp.float32)
         wide[1, rows] = k.astype(jnp.float32)
         wide[2, rows] = v.astype(jnp.float32)
@@ -154,12 +172,14 @@
     mid = branch(q, k, v, mid_ref[...])
     merged = merge((acc_ref[kept, :], top_ref[kept, :], total_ref[kept, :]), mid)
     acc_ref[kept, :], top_ref[kept, :], total_ref[kept, :] = merged
-    out_ref[...] = (acc_ref[...] / total_ref[...]).astype(jnp.bfloat16).reshape(PEERS, ROWS, DH)
+    for p, n in enumerate(ORDER_OUT):
+        rows = slice(n * ROWS, (n + 1) * ROWS)
+        out_ref[p] = (acc_ref[rows] / total_ref[rows]).astype(jnp.bfloat16)
     far = pl.ds(offset_of(offsets_ref, 1), KEPT, stride=R2)
-    far_ref[0] = acc_ref[far, :]
-    far_ref[1] = top_ref[far, :]
-    far_ref[2] = total_ref[far, :]
-    far_ref[3] = wide[0, far, :]
+    parts = acc_ref[far, :], top_ref[far, :], total_ref[far, :], wide[0, far, :]
+    for n, part in enumerate(parts):
+        for m, pair in enumerate(PAIRS_OUT):
+            far_ref[n, m : m + 1] = part[pair : pair + 1]
 
 
 def far_kernel(offsets_ref, kv_ref, bias_ref, far_ref, in_ref, out_ref):
@@ -196,7 +216,7 @@
         compiler_params=params(),
         name="pack",
     )(*(pltpu.with_memory_space_constraint(t, pltpu.HBM) for t in given))
-    qkv = lax.all_to_all(packed, ("g", "x"), 0, 0, tiled=True)
+    qkv = lax.all_to_all(packed, ("g", "x"), 0, 0, axis_index_groups=[ORDER_IN], tiled=True)
     kept = pl.pallas_call(
         kept_kernel,
         out_shape=jax.ShapeDtypeStruct((PLANES, 2 * KEPT, DH), bf16),
@@ -205,7 +225,7 @@
         compiler_params=params(),
         name="kept",
     )(picks, qkv.reshape(KEPT, 2, 3 * ROWS, DH))
-    kept = lax.all_to_all(kept, "z", 0, 0, tiled=True)
+    kept = lax.all_to_all(kept, "z", 0, 0, axis_index_groups=[RING], tiled=True)
     near_bias, mid_bias, far_bias = pl.pallas_call(
         bias_kernel,
         out_shape=(
@@ -244,7 +264,14 @@
         compiler_params=params(),
         name="far",
     )(picks, kept, far_bias, far_parts, local.reshape(KEPT, 2, ROWS, DH))
-    back = lax.all_to_all(merged.reshape(PEERS, ROWS, DH), ("g", "x"), 0, 0, tiled=True)
+    back = lax.all_to_all(
+        merged.reshape(PEERS, ROWS, DH),
+        ("g", "x"),
+        0,
+        0,
+        axis_index_groups=[ORDER_OUT],
+        tiled=True,
+    )
     return pl.pallas_call(
         unpack_kernel,
         out_shape=jax.ShapeDtypeStruct((ROWS, PEERS * DH), bf16),

time: 68.6 us -> 62.9 us (0.917)
  waiting for transfers between devices: 9.81 us -> 4.08 us
  blocking collectives: 39.2 us -> 38 us
  starting transfers between devices: 13.8 us -> 15 us
    all_to_all x1, waiting for transfers between devices: 9.81 us -> 4.08 us  [on_device(): kept = lax.all_to_all(kept, 'z', 0, 0, axis_index_groups=[RING], tiled=True)]
    all_to_all x1, starting transfers between devices: 13.8 us -> 15 us  [on_device(): kept = lax.all_to_all(kept, 'z', 0, 0, axis_index_groups=[RING], tiled=True)]
    all_to_all x2, blocking collectives: 39.2 us -> 38 us  [the longest x1 24.4 us: on_device(): lax.all_to_all(packed, ('g', 'x'), 0, 0, axis_index_groups=[ORDER_IN], ti...]
where the time goes in v3:
time: 62.9 us; the launch traced here: 62.6 us
  blocking collectives  38 us (60%)
  starting transfers between devices  15 us (24%)
  Pallas kernels  5.38 us (9%)
  waiting for transfers between devices  4.08 us (6%)
    all_to_all x1, blocking collectives, on_device(): lax.all_to_all(packed, ('g', 'x'), 0, 0, axis_index_groups=[ORDER_IN], ti...  24.4 us
    all_to_all x1, starting transfers between devices, on_device(): kept = lax.all_to_all(kept, 'z', 0, 0, axis_index_groups=[RING], tiled=True)  15 us
    all_to_all x1, blocking collectives, on_device(): lax.all_to_all(merged.reshape(PEERS, ROWS, DH), ('g', 'x'), 0, 0, axis_in...  13.7 us
    all_to_all x1, waiting for transfers between devices, on_device(): kept = lax.all_to_all(kept, 'z', 0, 0, axis_index_groups=[RING], tiled=True)  4.08 us
  transfers between devices with their start and end apart: 1, of which 1 were waited for; matrix products, arithmetic and copies ran while one was open for 0% of the time, Pallas kernels for 3%

profile of v3, /device:TPU:1, one launch (start us, length us, event | category | flops | bytes accessed | tf_op | source)
XLA Modules:
  0.0 62.6 jit_solution(15551058909293113805)
XLA Ops:
  0.0 1.2 %pack.1 = (bf16[32,96,128]{2,1,0:T(8,128)(2,1)S(1)}, s32[2,8]{1,0:T(2,128)S(1)}) custom-call(bf16[32,4096]{1,0:T(8,128)(2,1)} %q_ref.1, bf16[32,4096]{1,0:T(8,128)(2,1)} %k_ref.1, bf16[32,4096]{1,0:T(8,128)(2,1)} %v_ref.1, s32[2,8]{1,0:T(2,128)} %offsets_ref.1), custom_call_target="tpu_custom_call" | custom-call | tf_op jit(solution)/shard_map/pack/pallas_call | solution.py:207
  1.3 24.4 %all_to_all.15.qkv_ref = bf16[32,96,128]{2,1,0:T(8,128)(2,1)S(1)} all-to-all(bf16[32,96,128]{2,1,0:T(8,128)(2,1)S(1)} %get-tuple-element.13), channel_id=1, replica_groups={{27,26,25,24,19,18,17,16,11,10,9,8,3,2,1,0,31,30,29,28,23,22,21,20,15,1..., dimensions={0} | all-to-all | bytes 1572864 | tf_op jit(solution)/shard_map/all_to_all | solution.py:219
  25.6 0.9 %kept.1 = bf16[16,32,128]{2,1,0:T(8,128)(2,1)} custom-call(s32[2,8]{1,0:T(2,128)S(1)} %get-tuple-element.12.offsets_ref, bf16[16,2,96,128]{3,2,1,0:T(8,128)(2,1)S(1)} %bitcast.3), custom_call_target="tpu_custom_call" | custom-call | tf_op jit(solution)/shard_map/kept/pallas_call | solution.py:220
  26.5 0.0 copy-start
  26.5 15.0 %all-to-all-start.1 = ((bf16[16,32,128]{2,1,0:T(8,128)(2,1)}), bf16[16,32,128]{2,1,0:T(8,128)(2,1)S(1)}, u32[]{:S(2)}, u32[]{:S(2)}) async-start(bf16[16,32,128]{2,1,0:T(8,128)(2,1)} %kept.1), calls=%async_computation.1 | async-start | bytes 262144 | tf_op jit(solution)/shard_map/all_to_all | solution.py:228
  41.5 0.0 copy-done
  41.5 0.1 copy.7.table_ref
  41.6 1.1 %bias.1 = (f32[256,256]{1,0:T(8,128)S(1)}, f32[256,256]{1,0:T(8,128)S(1)}, f32[16,256]{1,0:T(8,128)S(1)}) custom-call(f32[32,8]{1,0:T(8,128)S(1)} %copy.7.table_ref), custom_call_target="tpu_custom_call" | custom-call | tf_op jit(solution)/shard_map/bias/pallas_call | solution.py:229
  42.7 1.0 %local.1 = (bf16[32,32,128]{2,1,0:T(8,128)(2,1)S(1)}, f32[4,16,128]{2,1,0:T(8,128)S(1)}) custom-call(s32[2,8]{1,0:T(2,128)S(1)} %get-tuple-element.12.offsets_ref, bf16[32,96,128]{2,1,0:T(8,128)(2,1)S(1)} %all_to_all.15.qkv_ref, f32[256,256]{1,0:T(8,128)S(1)} %get-tuple-element.15.near_ref, f32[256,256]{1,0:T(8,128)S(1)} %get-tuple-element.16.mid_ref), custom_call_target="tpu_custom_call" | custom-call | tf_op jit(solution)/shard_map/local/pallas_call | solution.py:241
  43.7 4.1 %all-to-all-done.1.kv_ref = bf16[16,32,128]{2,1,0:T(8,128)(2,1)S(1)} async-done(((bf16[16,32,128]{2,1,0:T(8,128)(2,1)}), bf16[16,32,128]{2,1,0:T(8,128)(2,1)S(1)}, u32[]{:S(2)}, u32[]{:S(2)}) %all-to-all-start.1) | async-done | bytes 131104 | tf_op jit(solution)/shard_map/all_to_all | solution.py:228
  47.8 0.4 far.1
  48.2 13.7 %all_to_all.16.in_ref = bf16[32,32,128]{2,1,0:T(8,128)(2,1)S(1)} all-to-all(bf16[32,32,128]{2,1,0:T(8,128)(2,1)S(1)} %bitcast.5), channel_id=1, replica_groups={{0,1,2,3,8,9,10,11,16,17,18,19,24,25,26,27,4,5,6,7,12,13,14,15,20,21,22..., dimensions={0} | all-to-all | bytes 524288 | tf_op jit(solution)/shard_map/all_to_all | solution.py:267
  61.8 0.8 %unpack.1 = bf16[32,4096]{1,0:T(8,128)(2,1)} custom-call(bf16[32,32,128]{2,1,0:T(8,128)(2,1)S(1)} %all_to_all.16.in_ref), custom_call_target="tpu_custom_call" | custom-call | tf_op jit(solution)/shard_map/unpack/pallas_call | solution.py:275
Async XLA Ops:
  26.5 15.0 %copy-start = (f32[32,8]{0,1:T(8,128)S(1)}, f32[32,8]{0,1:T(8,128)}, u32[]{:S(2)}) copy-start(f32[32,8]{0,1:T(8,128)} %param.8) | copy-start | bytes 3076
  26.5 21.3 %all-to-all-start.1 = ((bf16[16,32,128]{2,1,0:T(8,128)(2,1)}), bf16[16,32,128]{2,1,0:T(8,128)(2,1)S(1)}, u32[]{:S(2)}, u32[]{:S(2)}) async-start(bf16[16,32,128]{2,1,0:T(8,128)(2,1)} %kept.1), calls=%async_computation.1 | async-start | bytes 262144 | tf_op jit(solution)/shard_map/all_to_all | solution.py:228

commit v4 on v3

--- a/solution.py
+++ b/solution.py
@@ -20,7 +20,9 @@
 ROWS = 32
 SEG = PEERS * ROWS
 KEPT = SEG // R2
-RING = [8, 0, 1, 15, 2, 14, 3, 13, 4, 12, 5, 11, 6, 10, 7, 9]
+HALF = PLANES // 2
+LOW = [5, 0, 1, 2, 3, 4, 6, 7]
+HIGH = [11, 8, 9, 10, 12, 13, 14, 15]
 ORDER_IN = [(2 * y + c) * LANES + x for c in (0, 1) for y in (3, 2, 1, 0) for x in (3, 2, 1, 0)]
 ORDER_OUT = [(2 * y + c) * LANES + x for c in (0, 1) for y in (0, 1, 2, 3) for x in (0, 1, 2, 3)]
 PAIRS_IN = [n // 2 for n in ORDER_IN[::2]]
@@ -102,14 +104,18 @@
     mid_ref[...] = spread(line(R1), SPAN)
     row = lax.broadcasted_iota(jnp.int32, (KEPT, SPAN), 0)
     column = lax.broadcasted_iota(jnp.int32, (KEPT, SPAN), 1)
-    plane = jnp.zeros((KEPT, SPAN), jnp.int32)
-    for n in range(PLANES):
-        plane = jnp.where(column // KEPT == n, RING[n], plane)
+    here = lax.axis_index("z")
+    plane = jnp.full((KEPT, SPAN), PLANES, jnp.int32)
+    for n in range(HALF):
+        own = jnp.where(here < HALF, LOW[n], HIGH[n])
+        other = jnp.where(here < HALF, PLANES, LOW[n])
+        plane = jnp.where(column // KEPT == n, own, plane)
+        plane = jnp.where(column // KEPT == n + HALF, other, plane)
     query, key = jnp.zeros((KEPT, SPAN), jnp.int32), jnp.zeros((KEPT, SPAN), jnp.int32)
     for n in range(KEPT):
         query = jnp.where(row == n, PAIRS_OUT[n], query)
         key = jnp.where(column % KEPT == n, PAIRS_IN[n], key)
-    apart = (lax.axis_index("z") - plane) * KEPT + query - key
+    apart = (here - plane) * KEPT + query - key
     far_ref[...] = jnp.where(apart >= 0, value_at(apart * R2), NEG)
 
 
@@ -126,7 +132,7 @@
     pick = offset_of(offsets_ref, 1)
     keys = kept_tile(qkv_ref, 1, pick).astype(jnp.bfloat16)
     values = kept_tile(qkv_ref, 2, pick).astype(jnp.bfloat16)
-    for z in range(PLANES):
+    for z in range(HALF):
         out_ref[z, 0:KEPT] = keys
         out_ref[z, KEPT : 2 * KEPT] = values
 
@@ -182,11 +188,14 @@
             far_ref[n, m : m + 1] = part[pair : pair + 1]
 
 
-def far_kernel(offsets_ref, kv_ref, bias_ref, far_ref, in_ref, out_ref):
+def far_kernel(offsets_ref, bias_ref, far_ref, *refs):
+    *kv_refs, in_ref, out_ref = refs
     q = far_ref[3].astype(jnp.bfloat16)
-    k = kv_ref[:, 0:KEPT].reshape(SPAN, DH)
-    v = kv_ref[:, KEPT : 2 * KEPT].reshape(SPAN, DH)
-    far = branch(q, k, v, bias_ref[...])
+    kv = jnp.concatenate([ref[...] for ref in kv_refs], axis=0)
+    count = kv.shape[0] * KEPT
+    k = kv[:, 0:KEPT].reshape(count, DH)
+    v = kv[:, KEPT : 2 * KEPT].reshape(count, DH)
+    far = branch(q, k, v, bias_ref[:, 0:count])
     acc, _, total = merge((far_ref[0], far_ref[1], far_ref[2]), far)
     row = (acc / total).astype(jnp.bfloat16).astype(jnp.float32)
     out_ref[...] = in_ref[...]
@@ -216,61 +225,95 @@
         compiler_params=params(),
         name="pack",
     )(*(pltpu.with_memory_space_constraint(t, pltpu.HBM) for t in given))
+    is_low = lax.axis_index("z") < HALF
+    packed, is_low = lax.optimization_barrier((packed, is_low))
     qkv = lax.all_to_all(packed, ("g", "x"), 0, 0, axis_index_groups=[ORDER_IN], tiled=True)
     kept = pl.pallas_call(
         kept_kernel,
-        out_shape=jax.ShapeDtypeStruct((PLANES, 2 * KEPT, DH), bf16),
+        out_shape=jax.ShapeDtypeStruct((HALF, 2 * KEPT, DH), bf16),
         in_specs=[VMEM, VMEM],
         out_specs=VMEM,
         compiler_params=params(),
         name="kept",
     )(picks, qkv.reshape(KEPT, 2, 3 * ROWS, DH))
-    kept = lax.all_to_all(kept, "z", 0, 0, axis_index_groups=[RING], tiled=True)
-    near_bias, mid_bias, far_bias = pl.pallas_call(
-        bias_kernel,
-        out_shape=(
-            jax.ShapeDtypeStruct((SPAN, SPAN), f32),
-            jax.ShapeDtypeStruct((SPAN, SPAN), f32),
-            jax.ShapeDtypeStruct((KEPT, SPAN), f32),
-        ),
-        in_specs=[SMEM],
-        out_specs=(VMEM, VMEM, VMEM),
-        compiler_params=params(),
-        name="bias",
-    )(rel_bias)
-    local, far_parts = pl.pallas_call(
-        local_kernel,
-        out_shape=(
-            jax.ShapeDtypeStruct((PEERS, ROWS, DH), bf16),
-            jax.ShapeDtypeStruct((4, KEPT, DH), f32),
-        ),
-        in_specs=[VMEM] * 4,
-        out_specs=(VMEM, VMEM),
-        scratch_shapes=[
-            pltpu.VMEM((3, SEG, DH), f32),
-            pltpu.VMEM((SEG, DH), f32),
-            pltpu.VMEM((SEG, DH), f32),
-            pltpu.VMEM((SEG, DH), f32),
-        ],
-        compiler_params=params(),
-        name="local",
-    )(picks, qkv, near_bias, mid_bias)
-    merged = pl.pallas_call(
-        far_kernel,
-        out_shape=jax.ShapeDtypeStruct((KEPT, 2, ROWS, DH), bf16),
-        in_specs=[VMEM] * 5,
-        out_specs=VMEM,
-        input_output_aliases={4: 0},
-        compiler_params=params(),
-        name="far",
-    )(picks, kept, far_bias, far_parts, local.reshape(KEPT, 2, ROWS, DH))
-    back = lax.all_to_all(
-        merged.reshape(PEERS, ROWS, DH),
-        ("g", "x"),
-        0,
-        0,
-        axis_index_groups=[ORDER_OUT],
-        tiled=True,
+    def exchange(block):
+        return lax.all_to_all(block, "z", 0, 0, axis_index_groups=[LOW, HIGH], tiled=True)
+
+    def local(qkv, rel_bias):
+        near_bias, mid_bias, far_bias = pl.pallas_call(
+            bias_kernel,
+            out_shape=(
+                jax.ShapeDtypeStruct((SPAN, SPAN), f32),
+                jax.ShapeDtypeStruct((SPAN, SPAN), f32),
+                jax.ShapeDtypeStruct((KEPT, SPAN), f32),
+            ),
+            in_specs=[SMEM],
+            out_specs=(VMEM, VMEM, VMEM),
+            compiler_params=params(),
+            name="bias",
+        )(rel_bias)
+        rows, far_parts = pl.pallas_call(
+            local_kernel,
+            out_shape=(
+                jax.ShapeDtypeStruct((PEERS, ROWS, DH), bf16),
+                jax.ShapeDtypeStruct((4, KEPT, DH), f32),
+            ),
+            in_specs=[VMEM] * 4,
+            out_specs=(VMEM, VMEM),
+            scratch_shapes=[
+                pltpu.VMEM((3, SEG, DH), f32),
+                pltpu.VMEM((SEG, DH), f32),
+                pltpu.VMEM((SEG, DH), f32),
+                pltpu.VMEM((SEG, DH), f32),
+            ],
+            compiler_params=params(),
+            name="local",
+        )(picks, qkv, near_bias, mid_bias)
+        return rows, far_parts, far_bias
+
+    def finish(rows, far_parts, far_bias, *kv):
+        merged = pl.pallas_call(
+            far_kernel,
+            out_shape=jax.ShapeDtypeStruct((KEPT, 2, ROWS, DH), bf16),
+            in_specs=[VMEM] * (4 + len(kv)),
+            out_specs=VMEM,
+            input_output_aliases={3 + len(kv): 0},
+            compiler_params=params(),
+            name="far",
+        )(picks, far_bias, far_parts, *kv, rows.reshape(KEPT, 2, ROWS, DH))
+        return lax.all_to_all(
+            merged.reshape(PEERS, ROWS, DH),
+            ("g", "x"),
+            0,
+            0,
+            axis_index_groups=[ORDER_OUT],
+            tiled=True,
+        )
+
+    first, *parts = lax.cond(
+        is_low,
+        lambda block, *rest: (exchange(block), *local(*rest)),
+        lambda block, *rest: (block, *local(*rest)),
+        kept,
+        qkv,
+        rel_bias,
+    )
+    lower = lax.ppermute(first, "z", [(z, PLANES - 1 - z) for z in range(HALF)])
+    later = lax.cond(
+        is_low,
+        lambda first, kept, *parts: finish(*parts, first),
+        lambda first, kept, *parts: jnp.pad(exchange(kept), ((0, PEERS - HALF), (0, 0), (0, 0))),
+        first,
+        kept,
+        *parts,
+    )
+    back = lax.cond(
+        is_low,
+        lambda later, lower, *parts: later,
+        lambda later, lower, *parts: finish(*parts, later[:HALF], lower),
+        later,
+        lower,
+        *parts,
     )
     return pl.pallas_call(
         unpack_kernel,

time: 62.9 us -> 59.1 us (0.940)
  blocking collectives: 38 us -> 15 us
  starting transfers between devices: 15 us -> 23.9 us
  waiting for transfers between devices: 4.08 us -> 12.6 us
  Pallas kernels: 5.38 us -> 6.48 us
    all_to_all x2 -> x1, blocking collectives: 38 us -> 15 us  [finish(): lax.all_to_all(merged.reshape(PEERS, ROWS, DH), ('g', 'x'), 0, 0, axis_in...]
    all_to_all x1 -> x2, waiting for transfers between devices: 4.08 us -> 12.6 us  [the longest x1 11.2 us: on_device(): lax.all_to_all(packed, ('g', 'x'), 0, 0, axis_index_groups=[ORDER_IN], ti...]
    all_to_all x1 -> x2, starting transfers between devices: 15 us -> 22.6 us  [the longest x1 13.4 us: on_device(): lax.all_to_all(packed, ('g', 'x'), 0, 0, axis_index_groups=[ORDER_IN], ti...]
    ppermute x0 -> x1, starting transfers between devices: none -> 1.28 us  [on_device(): lower = lax.ppermute(first, 'z', [(z, PLANES - 1 - z) for z in range(HALF)])]
    pallas_call x1, Pallas kernels: 1.25 us -> 2.15 us  [on_device(): pl.pallas_call(pack_kernel, out_shape=(jax.ShapeDtypeStruct((PEERS, 3 * R...]
  transfers between devices with their start and end apart: 1 -> 3, of which waited for: 1 -> 2; matrix products, arithmetic and copies ran while one was open for 0% -> 0% of each run, Pallas kernels for 3% -> 6%
where the time goes in v4:
time: 59.1 us; the launch traced here: 58.7 us
  starting transfers between devices  23.9 us (40%)
  blocking collectives  15 us (25%)
  waiting for transfers between devices  12.6 us (21%)
  Pallas kernels  6.48 us (11%)
    all_to_all x1, blocking collectives, finish(): lax.all_to_all(merged.reshape(PEERS, ROWS, DH), ('g', 'x'), 0, 0, axis_in...  15 us
    all_to_all x1, starting transfers between devices, on_device(): lax.all_to_all(packed, ('g', 'x'), 0, 0, axis_index_groups=[ORDER_IN], ti...  13.4 us
    all_to_all x1, waiting for transfers between devices, on_device(): lax.all_to_all(packed, ('g', 'x'), 0, 0, axis_index_groups=[ORDER_IN], ti...  11.2 us
    all_to_all x1, starting transfers between devices, exchange(): lax.all_to_all(block, 'z', 0, 0, axis_index_groups=[LOW, HIGH], tiled=True)  9.24 us
    pallas_call x1, Pallas kernels, on_device(): pl.pallas_call(pack_kernel, out_shape=(jax.ShapeDtypeStruct((PEERS, 3 * R...  2.15 us
    all_to_all x1, waiting for transfers between devices, exchange(): lax.all_to_all(block, 'z', 0, 0, axis_index_groups=[LOW, HIGH], tiled=True)  1.38 us
    ppermute x1, starting transfers between devices, on_device(): lower = lax.ppermute(first, 'z', [(z, PLANES - 1 - z) for z in range(HALF)])  1.28 us
    pallas_call x1, Pallas kernels, finish(): pl.pallas_call(far_kernel, out_shape=jax.ShapeDtypeStruct((KEPT, 2, ROWS,...  1.24 us
  transfers between devices with their start and end apart: 3, of which 2 were waited for; matrix products, arithmetic and copies ran while one was open for 0% of the time, Pallas kernels for 6%

profile of v4, /device:TPU:1, one launch (start us, length us, event | category | flops | bytes accessed | tf_op | source)
XLA Modules:
  0.0 58.7 jit_solution(13311817623549592370)
XLA Ops:
  0.0 2.1 %pack.1 = (bf16[32,96,128]{2,1,0:T(8,128)(2,1)}, s32[2,8]{1,0:T(2,128)S(1)}) custom-call(bf16[32,4096]{1,0:T(8,128)(2,1)} %q_ref.1, bf16[32,4096]{1,0:T(8,128)(2,1)} %k_ref.1, bf16[32,4096]{1,0:T(8,128)(2,1)} %v_ref.1, s32[2,8]{1,0:T(2,128)} %offsets_ref.1), custom_call_target="tpu_custom_call" | custom-call | tf_op jit(solution)/shard_map/pack/pallas_call | solution.py:216
  2.2 13.4 %all-to-all-start.4 = ((bf16[32,96,128]{2,1,0:T(8,128)(2,1)}), bf16[32,96,128]{2,1,0:T(8,128)(2,1)S(1)}, u32[]{:S(2)}, u32[]{:S(2)}) async-start(bf16[32,96,128]{2,1,0:T(8,128)(2,1)} %get-tuple-element.91), calls=%async_computation.4 | async-start | bytes 1572864 | tf_op jit(solution)/shard_map/all_to_all | solution.py:230
  15.5 11.2 %all-to-all-done.4 = bf16[32,96,128]{2,1,0:T(8,128)(2,1)S(1)} async-done(((bf16[32,96,128]{2,1,0:T(8,128)(2,1)}), bf16[32,96,128]{2,1,0:T(8,128)(2,1)S(1)}, u32[]{:S(2)}, u32[]{:S(2)}) %all-to-all-start.4) | async-done | bytes 786464 | tf_op jit(solution)/shard_map/all_to_all | solution.py:230
  26.8 0.0 copy-start
  26.8 0.2 kept.1
  27.0 0.5 copy-done
  27.5 12.8 %conditional.3 = (bf16[8,32,128]{2,1,0:T(8,128)(2,1)}, bf16[32,32,128]{2,1,0:T(8,128)(2,1)S(1)}, f32[4,16,128]{2,1,0:T(8,128)S(1)}, f32[16,256]{1,0:T(8,128)S(1)}) conditional(s32[]{:T(128)} %convert_element_type.4, (f32[32,8]{0,1:T(8,128)S(1)}, s32[2,8]{1,0:T(2,128)S(1)}, bf16[32,96,128]{2,1,0:T(8,128)(2,1)S(1)}, ...), branch_computations={%region_0.0_spmd, %region_1.0_spmd} | conditional | bytes 198720 | solution.py:293
  27.5 9.2 %all-to-all-start = ((bf16[8,32,128]{2,1,0:T(8,128)(2,1)S(1)}), bf16[8,32,128]{2,1,0:T(8,128)(2,1)}, u32[]{:S(2)}, u32[]{:S(2)}) async-start(bf16[8,32,128]{2,1,0:T(8,128)(2,1)S(1)} %get-tuple-element.60), calls=%async_computation | async-start | bytes 131072 | tf_op jit(solution)/shard_map/cond/branch_1_fun/all_to_all | solution.py:240
  36.7 0.1 copy.9.table_ref
  36.8 1.1 %bias.3 = (f32[256,256]{1,0:T(8,128)S(1)}, f32[256,256]{1,0:T(8,128)S(1)}, f32[16,256]{1,0:T(8,128)S(1)}) custom-call(f32[32,8]{1,0:T(8,128)S(1)} %copy.9.table_ref), custom_call_target="tpu_custom_call" | custom-call | tf_op jit(solution)/shard_map/cond/branch_1_fun/bias/pallas_call | solution.py:243
  37.9 1.0 %local.3 = (bf16[32,32,128]{2,1,0:T(8,128)(2,1)S(1)}, f32[4,16,128]{2,1,0:T(8,128)S(1)}) custom-call(s32[2,8]{1,0:T(2,128)S(1)} %get-tuple-element.61.offsets_ref, bf16[32,96,128]{2,1,0:T(8,128)(2,1)S(1)} %get-tuple-element.62.qkv_ref, f32[256,256]{1,0:T(8,128)S(1)} %get-tuple-element.64.near_ref, f32[256,256]{1,0:T(8,128)S(1)} %get-tuple-element.65.mid_ref), custom_call_target="tpu_custom_call" | custom-call | tf_op jit(solution)/shard_map/cond/branch_1_fun/local/pallas_call | solution.py:255
  38.9 1.4 %all-to-all-done = bf16[8,32,128]{2,1,0:T(8,128)(2,1)} async-done(((bf16[8,32,128]{2,1,0:T(8,128)(2,1)S(1)}), bf16[8,32,128]{2,1,0:T(8,128)(2,1)}, u32[]{:S(2)}, u32[]{:S(2)}) %all-to-all-start) | async-done | bytes 65568 | tf_op jit(solution)/shard_map/cond/branch_1_fun/all_to_all | solution.py:240
  40.3 1.3 %collective-permute-start = (bf16[8,32,128]{2,1,0:T(8,128)(2,1)}, bf16[8,32,128]{2,1,0:T(8,128)(2,1)S(1)}, u32[]{:S(2)}, u32[]{:S(2)}) collective-permute-start(bf16[8,32,128]{2,1,0:T(8,128)(2,1)} %get-tuple-element.95), channel_id=1, source_target_pairs={{0,480},{32,448},{64,416},{96,384},{128,352},{160,320},{192,288},{... | collective-permute-start | bytes 196616 | tf_op jit(solution)/shard_map/ppermute | solution.py:301
  41.6 16.3 %conditional.4 = (bf16[32,32,128]{2,1,0:T(8,128)(2,1)S(1)}) conditional(s32[]{:T(128)} %convert_element_type.4, bf16[8,32,128]{2,1,0:T(8,128)(2,1)S(1)} %kept.1, (bf16[32,32,128]{2,1,0:T(8,128)(2,1)S(1)}, s32[2,8]{1,0:T(2,128)S(1)}, f32[16,256]{1,0:T(8,128)S(1)}, f32[4,16,128]{2,1,0:T(8,128)S(1)}, bf16[8,32,128]{2,1,0:T(8,128)(2,1)}) %tuple.29), branch_computations={%region_2.3_spmd, %region_3.4_spmd} | conditional | bytes 1048584 | solution.py:302
  41.6 1.2 %far.2 = bf16[16,2,32,128]{3,2,1,0:T(8,128)(2,1)S(1)} custom-call(s32[2,8]{1,0:T(2,128)S(1)} %get-tuple-element.69.offsets_ref, f32[16,256]{1,0:T(8,128)S(1)} %get-tuple-element.70.bias_ref, f32[4,16,128]{2,1,0:T(8,128)S(1)} %get-tuple-element.71.far_ref, bf16[8,32,128]{2,1,0:T(8,128)(2,1)} %get-tuple-element.72.refs_0_, ...), custom_call_target="tpu_custom_call", output_to_operand_aliasing={{}: (4, {})} | custom-call | tf_op jit(solution)/shard_map/cond/branch_1_fun/far/pallas_call | solution.py:275
  42.9 15.0 %all_to_all.22 = bf16[32,32,128]{2,1,0:T(8,128)(2,1)S(1)} all-to-all(bf16[32,32,128]{2,1,0:T(8,128)(2,1)S(1)} %bitcast.5), channel_id=1, replica_groups={{0,1,2,3,8,9,10,11,16,17,18,19,24,25,26,27,4,5,6,7,12,13,14,15,20,21,22..., dimensions={0} | all-to-all | bytes 524288 | tf_op jit(solution)/shard_map/cond/branch_1_fun/all_to_all | solution.py:284
  57.9 0.0 collective-permute-done
  57.9 0.8 %unpack.1 = bf16[32,4096]{1,0:T(8,128)(2,1)} custom-call(bf16[32,32,128]{2,1,0:T(8,128)(2,1)S(1)} %get-tuple-element.113.in_ref), custom_call_target="tpu_custom_call" | custom-call | tf_op jit(solution)/shard_map/unpack/pallas_call | solution.py:318
  (2 shorter events, 0.0 us)
Async XLA Ops:
  2.2 24.6 %all-to-all-start.4 = ((bf16[32,96,128]{2,1,0:T(8,128)(2,1)}), bf16[32,96,128]{2,1,0:T(8,128)(2,1)S(1)}, u32[]{:S(2)}, u32[]{:S(2)}) async-start(bf16[32,96,128]{2,1,0:T(8,128)(2,1)} %get-tuple-element.91), calls=%async_computation.4 | async-start | bytes 1572864 | tf_op jit(solution)/shard_map/all_to_all | solution.py:230
  26.8 0.7 %copy-start = (f32[32,8]{0,1:T(8,128)S(1)}, f32[32,8]{0,1:T(8,128)}, u32[]{:S(2)}) copy-start(f32[32,8]{0,1:T(8,128)} %param.14) | copy-start | bytes 3076
  27.5 12.8 %all-to-all-start = ((bf16[8,32,128]{2,1,0:T(8,128)(2,1)S(1)}), bf16[8,32,128]{2,1,0:T(8,128)(2,1)}, u32[]{:S(2)}, u32[]{:S(2)}) async-start(bf16[8,32,128]{2,1,0:T(8,128)(2,1)S(1)} %get-tuple-element.60), calls=%async_computation | async-start | bytes 131072 | tf_op jit(solution)/shard_map/cond/branch_1_fun/all_to_all | solution.py:240
  40.3 17.6 %collective-permute-start = (bf16[8,32,128]{2,1,0:T(8,128)(2,1)}, bf16[8,32,128]{2,1,0:T(8,128)(2,1)S(1)}, u32[]{:S(2)}, u32[]{:S(2)}) collective-permute-start(bf16[8,32,128]{2,1,0:T(8,128)(2,1)} %get-tuple-element.95), channel_id=1, source_target_pairs={{0,480},{32,448},{64,416},{96,384},{128,352},{160,320},{192,288},{... | collective-permute-start | bytes 196616 | tf_op jit(solution)/shard_map/ppermute | solution.py:301

commit v5 on v4

--- a/solution.py
+++ b/solution.py
@@ -48,8 +48,13 @@
     return starts
 
 
-def pack_kernel(q_ref, k_ref, v_ref, offsets_ref, out_ref, picks_ref, sems):
-    copies = [pltpu.make_async_copy(offsets_ref, picks_ref, sems.at[3])]
+def pack_kernel(
+    q_ref, k_ref, v_ref, offsets_ref, bias_ref, _, out_ref, picks_ref, table_ref, sems
+):
+    copies = [
+        pltpu.make_async_copy(offsets_ref, picks_ref, sems.at[3]),
+        pltpu.make_async_copy(bias_ref, table_ref, sems.at[4]),
+    ]
     for n, ref in enumerate((q_ref, k_ref, v_ref)):
         for g in range(GROUPS):
             for x in range(LANES):
@@ -88,9 +93,9 @@
     steps = jnp.where(lane == 0, 0, width - lane)
 
     def value_at(distance):
-        value = jnp.full(distance.shape, table_ref[0, head], jnp.float32)
+        value = jnp.full(distance.shape, table_ref[head, 0], jnp.float32)
         for n in range(1, BUCKETS):
-            value = jnp.where(distance >= starts[n], table_ref[n, head], value)
+            value = jnp.where(distance >= starts[n], table_ref[head, n], value)
         return value
 
     def line(stride):
@@ -212,21 +217,21 @@
 
 def on_device(queries, key_rows, value_rows, rel_bias, offsets):
     bf16, f32 = jnp.bfloat16, jnp.float32
-    given = (queries, key_rows, value_rows, offsets)
-    packed, picks = pl.pallas_call(
+    is_low = lax.axis_index("z") < HALF
+    given = (queries, key_rows, value_rows, offsets, rel_bias.T, is_low.astype(jnp.int32)[None])
+    packed, picks, table = pl.pallas_call(
         pack_kernel,
         out_shape=(
             jax.ShapeDtypeStruct((PEERS, 3 * ROWS, DH), bf16),
             jax.ShapeDtypeStruct(offsets.shape, offsets.dtype),
+            jax.ShapeDtypeStruct(rel_bias.T.shape, f32),
         ),
-        in_specs=[HBM] * 4,
-        out_specs=(VMEM, VMEM),
-        scratch_shapes=[pltpu.SemaphoreType.DMA((4,))],
+        in_specs=[HBM] * 6,
+        out_specs=(VMEM, VMEM, VMEM),
+        scratch_shapes=[pltpu.SemaphoreType.DMA((5,))],
         compiler_params=params(),
         name="pack",
     )(*(pltpu.with_memory_space_constraint(t, pltpu.HBM) for t in given))
-    is_low = lax.axis_index("z") < HALF
-    packed, is_low = lax.optimization_barrier((packed, is_low))
     qkv = lax.all_to_all(packed, ("g", "x"), 0, 0, axis_index_groups=[ORDER_IN], tiled=True)
     kept = pl.pallas_call(
         kept_kernel,
@@ -239,7 +244,7 @@
     def exchange(block):
         return lax.all_to_all(block, "z", 0, 0, axis_index_groups=[LOW, HIGH], tiled=True)
 
-    def local(qkv, rel_bias):
+    def local(qkv, table):
         near_bias, mid_bias, far_bias = pl.pallas_call(
             bias_kernel,
             out_shape=(
@@ -251,7 +256,7 @@
             out_specs=(VMEM, VMEM, VMEM),
             compiler_params=params(),
             name="bias",
-        )(rel_bias)
+        )(table)
         rows, far_parts = pl.pallas_call(
             local_kernel,
             out_shape=(
@@ -293,10 +298,10 @@
     first, *parts = lax.cond(
         is_low,
         lambda block, *rest: (exchange(block), *local(*rest)),
-        lambda block, *rest: (block, *local(*rest)),
+        lambda block, *rest: (jnp.zeros_like(block), *local(*rest)),
         kept,
         qkv,
-        rel_bias,
+        table,
     )
     lower = lax.ppermute(first, "z", [(z, PLANES - 1 - z) for z in range(HALF)])
     later = lax.cond(

time: 59.1 us -> 57.2 us (0.968)
  blocking collectives: 15 us -> 39.3 us
  starting transfers between devices: 23.9 us -> 10.4 us
  waiting for transfers between devices: 12.6 us -> 1.66 us
  Pallas kernels: 6.48 us -> 5.4 us
    all_to_all x0 -> x1, blocking collectives: none -> 24.4 us  [on_device(): lax.all_to_all(packed, ('g', 'x'), 0, 0, axis_index_groups=[ORDER_IN], ti...]
    all_to_all x1 -> x0, starting transfers between devices: 13.4 us -> none  [on_device(): lax.all_to_all(packed, ('g', 'x'), 0, 0, axis_index_groups=[ORDER_IN], ti...]
    all_to_all x1 -> x0, waiting for transfers between devices: 11.2 us -> none  [on_device(): lax.all_to_all(packed, ('g', 'x'), 0, 0, axis_index_groups=[ORDER_IN], ti...]
    pallas_call x1, Pallas kernels: 2.15 us -> 1.26 us  [on_device(): pl.pallas_call(pack_kernel, out_shape=(jax.ShapeDtypeStruct((PEERS, 3 * R...]
  transfers between devices with their start and end apart: 3 -> 2, of which waited for: 2 -> 1; matrix products, arithmetic and copies ran while one was open for 0% -> 0% of each run, Pallas kernels for 6% -> 6%
where the time goes in v5:
time: 57.2 us; the launch traced here: 56.9 us
  blocking collectives  39.3 us (69%)
  starting transfers between devices  10.4 us (18%)
  Pallas kernels  5.4 us (9%)
  waiting for transfers between devices  1.66 us (3%)
    all_to_all x1, blocking collectives, on_device(): lax.all_to_all(packed, ('g', 'x'), 0, 0, axis_index_groups=[ORDER_IN], ti...  24.4 us
    all_to_all x1, blocking collectives, finish(): lax.all_to_all(merged.reshape(PEERS, ROWS, DH), ('g', 'x'), 0, 0, axis_in...  15 us
    all_to_all x1, starting transfers between devices, exchange(): lax.all_to_all(block, 'z', 0, 0, axis_index_groups=[LOW, HIGH], tiled=True)  9.1 us
    all_to_all x1, waiting for transfers between devices, exchange(): lax.all_to_all(block, 'z', 0, 0, axis_index_groups=[LOW, HIGH], tiled=True)  1.66 us
    ppermute x1, starting transfers between devices, on_device(): lower = lax.ppermute(first, 'z', [(z, PLANES - 1 - z) for z in range(HALF)])  1.28 us
    pallas_call x1, Pallas kernels, on_device(): pl.pallas_call(pack_kernel, out_shape=(jax.ShapeDtypeStruct((PEERS, 3 * R...  1.26 us
    pallas_call x1, Pallas kernels, finish(): pl.pallas_call(far_kernel, out_shape=jax.ShapeDtypeStruct((KEPT, 2, ROWS,...  1.24 us
  transfers between devices with their start and end apart: 2, of which 1 were waited for; matrix products, arithmetic and copies ran while one was open for 0% of the time, Pallas kernels for 6%

profile of v5, /device:TPU:1, one launch (start us, length us, event | category | flops | bytes accessed | tf_op | source)
XLA Modules:
  0.0 56.9 jit_solution(2471922744054549398)
XLA Ops:
  0.0 1.3 %pack.1 = (bf16[32,96,128]{2,1,0:T(8,128)(2,1)S(1)}, s32[2,8]{1,0:T(2,128)S(1)}, f32[8,32]{1,0:T(8,128)S(1)}) custom-call(bf16[32,4096]{1,0:T(8,128)(2,1)} %q_ref.1, bf16[32,4096]{1,0:T(8,128)(2,1)} %k_ref.1, bf16[32,4096]{1,0:T(8,128)(2,1)} %v_ref.1, s32[2,8]{1,0:T(2,128)} %offsets_ref.1, f32[8,32]{1,0:T(8,128)} %bitcast.12, s32[1]{0:T(128)} %bitcast.5._), custom_call_target="tpu_custom_call" | custom-call | tf_op jit(solution)/shard_map/pack/pallas_call | solution.py:222
  1.3 24.4 %all_to_all.24 = bf16[32,96,128]{2,1,0:T(8,128)(2,1)S(1)} all-to-all(bf16[32,96,128]{2,1,0:T(8,128)(2,1)S(1)} %get-tuple-element.85), channel_id=1, replica_groups={{27,26,25,24,19,18,17,16,11,10,9,8,3,2,1,0,31,30,29,28,23,22,21,20,15,1..., dimensions={0} | all-to-all | bytes 1572864 | tf_op jit(solution)/shard_map/all_to_all | solution.py:235
  25.7 0.2 kept.1
  25.9 12.7 %conditional.3 = (bf16[8,32,128]{2,1,0:T(8,128)(2,1)}, bf16[32,32,128]{2,1,0:T(8,128)(2,1)S(1)}, f32[4,16,128]{2,1,0:T(8,128)S(1)}, f32[16,256]{1,0:T(8,128)S(1)}) conditional(s32[]{:T(128)} %convert_element_type.3, (f32[8,32]{1,0:T(8,128)S(1)}, s32[2,8]{1,0:T(2,128)S(1)}, bf16[32,96,128]{2,1,0:T(8,128)(2,1)S(1)}) %tuple.25, ...), branch_computations={%region_0.0_spmd, %region_1.0_spmd} | conditional | bytes 196672 | solution.py:298
  25.9 9.1 %all-to-all-start = ((bf16[8,32,128]{2,1,0:T(8,128)(2,1)S(1)}), bf16[8,32,128]{2,1,0:T(8,128)(2,1)}, u32[]{:S(2)}, u32[]{:S(2)}) async-start(bf16[8,32,128]{2,1,0:T(8,128)(2,1)S(1)} %get-tuple-element.57), calls=%async_computation | async-start | bytes 131072 | tf_op jit(solution)/shard_map/cond/branch_1_fun/all_to_all | solution.py:245
  35.0 0.9 %bias.3 = (f32[256,256]{1,0:T(8,128)S(1)}, f32[256,256]{1,0:T(8,128)S(1)}, f32[16,256]{1,0:T(8,128)S(1)}) custom-call(f32[8,32]{1,0:T(8,128)S(1)} %get-tuple-element.60.table_ref), custom_call_target="tpu_custom_call" | custom-call | tf_op jit(solution)/shard_map/cond/branch_1_fun/bias/pallas_call | solution.py:248
  35.9 1.0 %local.3 = (bf16[32,32,128]{2,1,0:T(8,128)(2,1)S(1)}, f32[4,16,128]{2,1,0:T(8,128)S(1)}) custom-call(s32[2,8]{1,0:T(2,128)S(1)} %get-tuple-element.58.offsets_ref, bf16[32,96,128]{2,1,0:T(8,128)(2,1)S(1)} %get-tuple-element.59.qkv_ref, f32[256,256]{1,0:T(8,128)S(1)} %get-tuple-element.61.near_ref, f32[256,256]{1,0:T(8,128)S(1)} %get-tuple-element.62.mid_ref), custom_call_target="tpu_custom_call" | custom-call | tf_op jit(solution)/shard_map/cond/branch_1_fun/local/pallas_call | solution.py:260
  36.9 1.7 %all-to-all-done = bf16[8,32,128]{2,1,0:T(8,128)(2,1)} async-done(((bf16[8,32,128]{2,1,0:T(8,128)(2,1)S(1)}), bf16[8,32,128]{2,1,0:T(8,128)(2,1)}, u32[]{:S(2)}, u32[]{:S(2)}) %all-to-all-start) | async-done | bytes 65568 | tf_op jit(solution)/shard_map/cond/branch_1_fun/all_to_all | solution.py:245
  38.6 1.3 %collective-permute-start = (bf16[8,32,128]{2,1,0:T(8,128)(2,1)}, bf16[8,32,128]{2,1,0:T(8,128)(2,1)S(1)}, u32[]{:S(2)}, u32[]{:S(2)}) collective-permute-start(bf16[8,32,128]{2,1,0:T(8,128)(2,1)} %get-tuple-element.90), channel_id=1, source_target_pairs={{0,480},{32,448},{64,416},{96,384},{128,352},{160,320},{192,288},{... | collective-permute-start | bytes 196616 | tf_op jit(solution)/shard_map/ppermute | solution.py:306
  39.9 16.3 %conditional.4 = (bf16[32,32,128]{2,1,0:T(8,128)(2,1)S(1)}) conditional(s32[]{:T(128)} %convert_element_type.3, bf16[8,32,128]{2,1,0:T(8,128)(2,1)S(1)} %kept.1, (bf16[32,32,128]{2,1,0:T(8,128)(2,1)S(1)}, s32[2,8]{1,0:T(2,128)S(1)}, f32[16,256]{1,0:T(8,128)S(1)}, f32[4,16,128]{2,1,0:T(8,128)S(1)}, bf16[8,32,128]{2,1,0:T(8,128)(2,1)}) %tuple.27), branch_computations={%region_2.3_spmd, %region_3.4_spmd} | conditional | bytes 1048584 | solution.py:307
  39.9 1.2 %far.2 = bf16[16,2,32,128]{3,2,1,0:T(8,128)(2,1)S(1)} custom-call(s32[2,8]{1,0:T(2,128)S(1)} %get-tuple-element.66.offsets_ref, f32[16,256]{1,0:T(8,128)S(1)} %get-tuple-element.67.bias_ref, f32[4,16,128]{2,1,0:T(8,128)S(1)} %get-tuple-element.68.far_ref, bf16[8,32,128]{2,1,0:T(8,128)(2,1)} %get-tuple-element.69.refs_0_, ...), custom_call_target="tpu_custom_call", output_to_operand_aliasing={{}: (4, {})} | custom-call | tf_op jit(solution)/shard_map/cond/branch_1_fun/far/pallas_call | solution.py:280
  41.2 15.0 %all_to_all.22 = bf16[32,32,128]{2,1,0:T(8,128)(2,1)S(1)} all-to-all(bf16[32,32,128]{2,1,0:T(8,128)(2,1)S(1)} %bitcast.7), channel_id=1, replica_groups={{0,1,2,3,8,9,10,11,16,17,18,19,24,25,26,27,4,5,6,7,12,13,14,15,20,21,22..., dimensions={0} | all-to-all | bytes 524288 | tf_op jit(solution)/shard_map/cond/branch_1_fun/all_to_all | solution.py:289
  56.1 0.0 collective-permute-done
  56.1 0.8 %unpack.1 = bf16[32,4096]{1,0:T(8,128)(2,1)} custom-call(bf16[32,32,128]{2,1,0:T(8,128)(2,1)S(1)} %get-tuple-element.100.in_ref), custom_call_target="tpu_custom_call" | custom-call | tf_op jit(solution)/shard_map/unpack/pallas_call | solution.py:323
  (2 shorter events, 0.0 us)
Async XLA Ops:
  25.9 12.7 %all-to-all-start = ((bf16[8,32,128]{2,1,0:T(8,128)(2,1)S(1)}), bf16[8,32,128]{2,1,0:T(8,128)(2,1)}, u32[]{:S(2)}, u32[]{:S(2)}) async-start(bf16[8,32,128]{2,1,0:T(8,128)(2,1)S(1)} %get-tuple-element.57), calls=%async_computation | async-start | bytes 131072 | tf_op jit(solution)/shard_map/cond/branch_1_fun/all_to_all | solution.py:245
  38.6 17.5 %collective-permute-start = (bf16[8,32,128]{2,1,0:T(8,128)(2,1)}, bf16[8,32,128]{2,1,0:T(8,128)(2,1)S(1)}, u32[]{:S(2)}, u32[]{:S(2)}) collective-permute-start(bf16[8,32,128]{2,1,0:T(8,128)(2,1)} %get-tuple-element.90), channel_id=1, source_target_pairs={{0,480},{32,448},{64,416},{96,384},{128,352},{160,320},{192,288},{... | collective-permute-start | bytes 196616 | tf_op jit(solution)/shard_map/ppermute | solution.py:306

commit v6 on v5

--- a/solution.py
+++ b/solution.py
@@ -21,13 +21,14 @@
 SEG = PEERS * ROWS
 KEPT = SEG // R2
 HALF = PLANES // 2
-LOW = [5, 0, 1, 2, 3, 4, 6, 7]
+LOW = [6, 0, 1, 2, 3, 4, 5, 7]
 HIGH = [11, 8, 9, 10, 12, 13, 14, 15]
-ORDER_IN = [(2 * y + c) * LANES + x for c in (0, 1) for y in (3, 2, 1, 0) for x in (3, 2, 1, 0)]
+ORDER_IN = [(2 * y + c) * LANES + x for c in (1, 0) for y in (3, 2, 1, 0) for x in (3, 2, 1, 0)]
 ORDER_OUT = [(2 * y + c) * LANES + x for c in (0, 1) for y in (0, 1, 2, 3) for x in (0, 1, 2, 3)]
 PAIRS_IN = [n // 2 for n in ORDER_IN[::2]]
 PAIRS_OUT = [n // 2 for n in ORDER_OUT[::2]]
 PLACE = {n: p for p, n in enumerate(ORDER_IN)}
+UPPER = [12, 13, 14, 15, 11, 10, 8, 9]
 NEG = -1e30
 SCALE = DH ** (-0.5)
 
@@ -303,7 +304,7 @@
         qkv,
         table,
     )
-    lower = lax.ppermute(first, "z", [(z, PLANES - 1 - z) for z in range(HALF)])
+    lower = lax.ppermute(first, "z", list(enumerate(UPPER)))
     later = lax.cond(
         is_low,
         lambda first, kept, *parts: finish(*parts, first),

time: 57.2 us -> 55.9 us (0.977)
  blocking collectives: 39.3 us -> 38 us
    all_to_all x1, blocking collectives: 15 us -> 13.9 us  [finish(): lax.all_to_all(merged.reshape(PEERS, ROWS, DH), ('g', 'x'), 0, 0, axis_in...]
where the time goes in v6:
time: 55.9 us; the launch traced here: 55.6 us
  blocking collectives  38 us (68%)
  starting transfers between devices  10.6 us (19%)
  Pallas kernels  5.4 us (10%)
  waiting for transfers between devices  1.43 us (3%)
    all_to_all x1, blocking collectives, on_device(): lax.all_to_all(packed, ('g', 'x'), 0, 0, axis_index_groups=[ORDER_IN], ti...  24.1 us
    all_to_all x1, blocking collectives, finish(): lax.all_to_all(merged.reshape(PEERS, ROWS, DH), ('g', 'x'), 0, 0, axis_in...  13.9 us
    all_to_all x1, starting transfers between devices, exchange(): lax.all_to_all(block, 'z', 0, 0, axis_index_groups=[LOW, HIGH], tiled=True)  9.34 us
    all_to_all x1, waiting for transfers between devices, exchange(): lax.all_to_all(block, 'z', 0, 0, axis_index_groups=[LOW, HIGH], tiled=True)  1.43 us
    ppermute x1, starting transfers between devices, on_device(): lower = lax.ppermute(first, 'z', list(enumerate(UPPER)))  1.28 us
    pallas_call x1, Pallas kernels, on_device(): pl.pallas_call(pack_kernel, out_shape=(jax.ShapeDtypeStruct((PEERS, 3 * R...  1.26 us
    pallas_call x1, Pallas kernels, finish(): pl.pallas_call(far_kernel, out_shape=jax.ShapeDtypeStruct((KEPT, 2, ROWS,...  1.24 us
  transfers between devices with their start and end apart: 2, of which 1 were waited for; matrix products, arithmetic and copies ran while one was open for 0% of the time, Pallas kernels for 6%

profile of v6, /device:TPU:1, one launch (start us, length us, event | category | flops | bytes accessed | tf_op | source)
XLA Modules:
  0.0 55.6 jit_solution(17238149399737468248)
XLA Ops:
  0.0 1.3 %pack.1 = (bf16[32,96,128]{2,1,0:T(8,128)(2,1)S(1)}, s32[2,8]{1,0:T(2,128)S(1)}, f32[8,32]{1,0:T(8,128)S(1)}) custom-call(bf16[32,4096]{1,0:T(8,128)(2,1)} %q_ref.1, bf16[32,4096]{1,0:T(8,128)(2,1)} %k_ref.1, bf16[32,4096]{1,0:T(8,128)(2,1)} %v_ref.1, s32[2,8]{1,0:T(2,128)} %offsets_ref.1, f32[8,32]{1,0:T(8,128)} %bitcast.12, s32[1]{0:T(128)} %bitcast.5._), custom_call_target="tpu_custom_call" | custom-call | tf_op jit(solution)/shard_map/pack/pallas_call | solution.py:223
  1.3 24.1 %all_to_all.24 = bf16[32,96,128]{2,1,0:T(8,128)(2,1)S(1)} all-to-all(bf16[32,96,128]{2,1,0:T(8,128)(2,1)S(1)} %get-tuple-element.85), channel_id=1, replica_groups={{31,30,29,28,23,22,21,20,15,14,13,12,7,6,5,4,27,26,25,24,19,18,17,16,11..., dimensions={0} | all-to-all | bytes 1572864 | tf_op jit(solution)/shard_map/all_to_all | solution.py:236
  25.3 0.2 kept.1
  25.6 12.7 %conditional.3 = (bf16[8,32,128]{2,1,0:T(8,128)(2,1)}, bf16[32,32,128]{2,1,0:T(8,128)(2,1)S(1)}, f32[4,16,128]{2,1,0:T(8,128)S(1)}, f32[16,256]{1,0:T(8,128)S(1)}) conditional(s32[]{:T(128)} %convert_element_type.3, (f32[8,32]{1,0:T(8,128)S(1)}, s32[2,8]{1,0:T(2,128)S(1)}, bf16[32,96,128]{2,1,0:T(8,128)(2,1)S(1)}) %tuple.25, ...), branch_computations={%region_0.0_spmd, %region_1.0_spmd} | conditional | bytes 196672 | solution.py:299
  25.6 9.3 %all-to-all-start = ((bf16[8,32,128]{2,1,0:T(8,128)(2,1)S(1)}), bf16[8,32,128]{2,1,0:T(8,128)(2,1)}, u32[]{:S(2)}, u32[]{:S(2)}) async-start(bf16[8,32,128]{2,1,0:T(8,128)(2,1)S(1)} %get-tuple-element.57), calls=%async_computation | async-start | bytes 131072 | tf_op jit(solution)/shard_map/cond/branch_1_fun/all_to_all | solution.py:246
  34.9 0.9 %bias.3 = (f32[256,256]{1,0:T(8,128)S(1)}, f32[256,256]{1,0:T(8,128)S(1)}, f32[16,256]{1,0:T(8,128)S(1)}) custom-call(f32[8,32]{1,0:T(8,128)S(1)} %get-tuple-element.60.table_ref), custom_call_target="tpu_custom_call" | custom-call | tf_op jit(solution)/shard_map/cond/branch_1_fun/bias/pallas_call | solution.py:249
  35.8 1.0 %local.3 = (bf16[32,32,128]{2,1,0:T(8,128)(2,1)S(1)}, f32[4,16,128]{2,1,0:T(8,128)S(1)}) custom-call(s32[2,8]{1,0:T(2,128)S(1)} %get-tuple-element.58.offsets_ref, bf16[32,96,128]{2,1,0:T(8,128)(2,1)S(1)} %get-tuple-element.59.qkv_ref, f32[256,256]{1,0:T(8,128)S(1)} %get-tuple-element.61.near_ref, f32[256,256]{1,0:T(8,128)S(1)} %get-tuple-element.62.mid_ref), custom_call_target="tpu_custom_call" | custom-call | tf_op jit(solution)/shard_map/cond/branch_1_fun/local/pallas_call | solution.py:261
  36.8 1.4 %all-to-all-done = bf16[8,32,128]{2,1,0:T(8,128)(2,1)} async-done(((bf16[8,32,128]{2,1,0:T(8,128)(2,1)S(1)}), bf16[8,32,128]{2,1,0:T(8,128)(2,1)}, u32[]{:S(2)}, u32[]{:S(2)}) %all-to-all-start) | async-done | bytes 65568 | tf_op jit(solution)/shard_map/cond/branch_1_fun/all_to_all | solution.py:246
  38.3 1.3 %collective-permute-start = (bf16[8,32,128]{2,1,0:T(8,128)(2,1)}, bf16[8,32,128]{2,1,0:T(8,128)(2,1)S(1)}, u32[]{:S(2)}, u32[]{:S(2)}) collective-permute-start(bf16[8,32,128]{2,1,0:T(8,128)(2,1)} %get-tuple-element.90), channel_id=1, source_target_pairs={{0,384},{32,416},{64,448},{96,480},{128,352},{160,320},{192,256},{... | collective-permute-start | bytes 196616 | tf_op jit(solution)/shard_map/ppermute | solution.py:307
  39.6 15.2 %conditional.4 = (bf16[32,32,128]{2,1,0:T(8,128)(2,1)S(1)}) conditional(s32[]{:T(128)} %convert_element_type.3, bf16[8,32,128]{2,1,0:T(8,128)(2,1)S(1)} %kept.1, (bf16[32,32,128]{2,1,0:T(8,128)(2,1)S(1)}, s32[2,8]{1,0:T(2,128)S(1)}, f32[16,256]{1,0:T(8,128)S(1)}, f32[4,16,128]{2,1,0:T(8,128)S(1)}, bf16[8,32,128]{2,1,0:T(8,128)(2,1)}) %tuple.27), branch_computations={%region_2.3_spmd, %region_3.4_spmd} | conditional | bytes 1048584 | solution.py:308
  39.6 1.2 %far.2 = bf16[16,2,32,128]{3,2,1,0:T(8,128)(2,1)S(1)} custom-call(s32[2,8]{1,0:T(2,128)S(1)} %get-tuple-element.66.offsets_ref, f32[16,256]{1,0:T(8,128)S(1)} %get-tuple-element.67.bias_ref, f32[4,16,128]{2,1,0:T(8,128)S(1)} %get-tuple-element.68.far_ref, bf16[8,32,128]{2,1,0:T(8,128)(2,1)} %get-tuple-element.69.refs_0_, ...), custom_call_target="tpu_custom_call", output_to_operand_aliasing={{}: (4, {})} | custom-call | tf_op jit(solution)/shard_map/cond/branch_1_fun/far/pallas_call | solution.py:281
  40.9 13.9 %all_to_all.22 = bf16[32,32,128]{2,1,0:T(8,128)(2,1)S(1)} all-to-all(bf16[32,32,128]{2,1,0:T(8,128)(2,1)S(1)} %bitcast.7), channel_id=1, replica_groups={{0,1,2,3,8,9,10,11,16,17,18,19,24,25,26,27,4,5,6,7,12,13,14,15,20,21,22..., dimensions={0} | all-to-all | bytes 524288 | tf_op jit(solution)/shard_map/cond/branch_1_fun/all_to_all | solution.py:290
  54.8 0.0 collective-permute-done
  54.8 0.8 %unpack.1 = bf16[32,4096]{1,0:T(8,128)(2,1)} custom-call(bf16[32,32,128]{2,1,0:T(8,128)(2,1)S(1)} %get-tuple-element.100.in_ref), custom_call_target="tpu_custom_call" | custom-call | tf_op jit(solution)/shard_map/unpack/pallas_call | solution.py:324
  (2 shorter events, 0.0 us)
Async XLA Ops:
  25.6 12.7 %all-to-all-start = ((bf16[8,32,128]{2,1,0:T(8,128)(2,1)S(1)}), bf16[8,32,128]{2,1,0:T(8,128)(2,1)}, u32[]{:S(2)}, u32[]{:S(2)}) async-start(bf16[8,32,128]{2,1,0:T(8,128)(2,1)S(1)} %get-tuple-element.57), calls=%async_computation | async-start | bytes 131072 | tf_op jit(solution)/shard_map/cond/branch_1_fun/all_to_all | solution.py:246
  38.3 16.5 %collective-permute-start = (bf16[8,32,128]{2,1,0:T(8,128)(2,1)}, bf16[8,32,128]{2,1,0:T(8,128)(2,1)S(1)}, u32[]{:S(2)}, u32[]{:S(2)}) collective-permute-start(bf16[8,32,128]{2,1,0:T(8,128)(2,1)} %get-tuple-element.90), channel_id=1, source_target_pairs={{0,384},{32,416},{64,448},{96,480},{128,352},{160,320},{192,256},{... | collective-permute-start | bytes 196616 | tf_op jit(solution)/shard_map/ppermute | solution.py:307

commit v7 on v6

--- a/solution.py
+++ b/solution.py
@@ -24,7 +24,7 @@
 LOW = [6, 0, 1, 2, 3, 4, 5, 7]
 HIGH = [11, 8, 9, 10, 12, 13, 14, 15]
 ORDER_IN = [(2 * y + c) * LANES + x for c in (1, 0) for y in (3, 2, 1, 0) for x in (3, 2, 1, 0)]
-ORDER_OUT = [(2 * y + c) * LANES + x for c in (0, 1) for y in (0, 1, 2, 3) for x in (0, 1, 2, 3)]
+ORDER_OUT = [(2 * y + c) * LANES + x for c in (1, 0) for y in (0, 1, 2, 3) for x in (0, 1, 2, 3)]
 PAIRS_IN = [n // 2 for n in ORDER_IN[::2]]
 PAIRS_OUT = [n // 2 for n in ORDER_OUT[::2]]
 PLACE = {n: p for p, n in enumerate(ORDER_IN)}
@@ -50,7 +50,7 @@
 
 
 def pack_kernel(
-    q_ref, k_ref, v_ref, offsets_ref, bias_ref, _, out_ref, picks_ref, table_ref, sems
+    q_ref, k_ref, v_ref, offsets_ref, bias_ref, _, out_ref, picks_ref, table_ref, __, sems
 ):
     copies = [
         pltpu.make_async_copy(offsets_ref, picks_ref, sems.at[3]),
@@ -220,15 +220,16 @@
     bf16, f32 = jnp.bfloat16, jnp.float32
     is_low = lax.axis_index("z") < HALF
     given = (queries, key_rows, value_rows, offsets, rel_bias.T, is_low.astype(jnp.int32)[None])
-    packed, picks, table = pl.pallas_call(
+    packed, picks, table, spare = pl.pallas_call(
         pack_kernel,
         out_shape=(
             jax.ShapeDtypeStruct((PEERS, 3 * ROWS, DH), bf16),
             jax.ShapeDtypeStruct(offsets.shape, offsets.dtype),
             jax.ShapeDtypeStruct(rel_bias.T.shape, f32),
+            jax.ShapeDtypeStruct((HALF, 2 * KEPT, DH), bf16),
         ),
         in_specs=[HBM] * 6,
-        out_specs=(VMEM, VMEM, VMEM),
+        out_specs=(VMEM, VMEM, VMEM, HBM),
         scratch_shapes=[pltpu.SemaphoreType.DMA((5,))],
         compiler_params=params(),
         name="pack",
@@ -298,9 +299,10 @@
 
     first, *parts = lax.cond(
         is_low,
-        lambda block, *rest: (exchange(block), *local(*rest)),
-        lambda block, *rest: (jnp.zeros_like(block), *local(*rest)),
+        lambda block, spare, *rest: (exchange(block), *local(*rest)),
+        lambda block, spare, *rest: (spare, *local(*rest)),
         kept,
+        spare,
         qkv,
         table,
     )

time: 55.9 us -> 55.6 us (level)
  no operation moved by 1% of the time
where the time goes in v7:
time: 55.6 us; the launch traced here: 55.3 us
  blocking collectives  37.7 us (68%)
  starting transfers between devices  10.6 us (19%)
  Pallas kernels  5.4 us (10%)
  waiting for transfers between devices  1.44 us (3%)
    all_to_all x1, blocking collectives, on_device(): lax.all_to_all(packed, ('g', 'x'), 0, 0, axis_index_groups=[ORDER_IN], ti...  24.1 us
    all_to_all x1, blocking collectives, finish(): lax.all_to_all(merged.reshape(PEERS, ROWS, DH), ('g', 'x'), 0, 0, axis_in...  13.6 us
    all_to_all x1, starting transfers between devices, exchange(): lax.all_to_all(block, 'z', 0, 0, axis_index_groups=[LOW, HIGH], tiled=True)  9.34 us
    all_to_all x1, waiting for transfers between devices, exchange(): lax.all_to_all(block, 'z', 0, 0, axis_index_groups=[LOW, HIGH], tiled=True)  1.43 us
    ppermute x1, starting transfers between devices, on_device(): lower = lax.ppermute(first, 'z', list(enumerate(UPPER)))  1.28 us
    pallas_call x1, Pallas kernels, on_device(): pl.pallas_call(pack_kernel, out_shape=(jax.ShapeDtypeStruct((PEERS, 3 * R...  1.26 us
    pallas_call x1, Pallas kernels, finish(): pl.pallas_call(far_kernel, out_shape=jax.ShapeDtypeStruct((KEPT, 2, ROWS,...  1.24 us
  transfers between devices with their start and end apart: 2, of which 1 were waited for; matrix products, arithmetic and copies ran while one was open for 0% of the time, Pallas kernels for 6%

profile of v7, /device:TPU:1, one launch (start us, length us, event | category | flops | bytes accessed | tf_op | source)
XLA Modules:
  0.0 55.3 jit_solution(2970695906512756604)
XLA Ops:
  0.0 1.3 %pack.1 = (bf16[32,96,128]{2,1,0:T(8,128)(2,1)S(1)}, s32[2,8]{1,0:T(2,128)S(1)}, f32[8,32]{1,0:T(8,128)S(1)}, bf16[8,32,128]{2,1,0:T(8,128)(2,1)}) custom-call(bf16[32,4096]{1,0:T(8,128)(2,1)} %q_ref.1, bf16[32,4096]{1,0:T(8,128)(2,1)} %k_ref.1, bf16[32,4096]{1,0:T(8,128)(2,1)} %v_ref.1, s32[2,8]{1,0:T(2,128)} %offsets_ref.1, f32[8,32]{1,0:T(8,128)} %bitcast.12, ...), custom_call_target="tpu_custom_call" | custom-call | tf_op jit(solution)/shard_map/pack/pallas_call | solution.py:223
  1.3 24.1 %all_to_all.24 = bf16[32,96,128]{2,1,0:T(8,128)(2,1)S(1)} all-to-all(bf16[32,96,128]{2,1,0:T(8,128)(2,1)S(1)} %get-tuple-element.89), channel_id=1, replica_groups={{31,30,29,28,23,22,21,20,15,14,13,12,7,6,5,4,27,26,25,24,19,18,17,16,11..., dimensions={0} | all-to-all | bytes 1572864 | tf_op jit(solution)/shard_map/all_to_all | solution.py:237
  25.3 0.2 kept.1
  25.6 12.7 %conditional.3 = (bf16[8,32,128]{2,1,0:T(8,128)(2,1)}, bf16[32,32,128]{2,1,0:T(8,128)(2,1)S(1)}, f32[4,16,128]{2,1,0:T(8,128)S(1)}, f32[16,256]{1,0:T(8,128)S(1)}) conditional(s32[]{:T(128)} %convert_element_type.3, (f32[8,32]{1,0:T(8,128)S(1)}, s32[2,8]{1,0:T(2,128)S(1)}, bf16[32,96,128]{2,1,0:T(8,128)(2,1)S(1)}, ...), branch_computations={%region_0.0_spmd, %region_1.0_spmd} | conditional | bytes 196672 | solution.py:300
  25.6 9.3 %all-to-all-start = ((bf16[8,32,128]{2,1,0:T(8,128)(2,1)S(1)}), bf16[8,32,128]{2,1,0:T(8,128)(2,1)}, u32[]{:S(2)}, u32[]{:S(2)}) async-start(bf16[8,32,128]{2,1,0:T(8,128)(2,1)S(1)} %get-tuple-element.60), calls=%async_computation | async-start | bytes 131072 | tf_op jit(solution)/shard_map/cond/branch_1_fun/all_to_all | solution.py:247
  34.9 0.9 %bias.3 = (f32[256,256]{1,0:T(8,128)S(1)}, f32[256,256]{1,0:T(8,128)S(1)}, f32[16,256]{1,0:T(8,128)S(1)}) custom-call(f32[8,32]{1,0:T(8,128)S(1)} %get-tuple-element.63.table_ref), custom_call_target="tpu_custom_call" | custom-call | tf_op jit(solution)/shard_map/cond/branch_1_fun/bias/pallas_call | solution.py:250
  35.8 1.0 %local.3 = (bf16[32,32,128]{2,1,0:T(8,128)(2,1)S(1)}, f32[4,16,128]{2,1,0:T(8,128)S(1)}) custom-call(s32[2,8]{1,0:T(2,128)S(1)} %get-tuple-element.61.offsets_ref, bf16[32,96,128]{2,1,0:T(8,128)(2,1)S(1)} %get-tuple-element.62.qkv_ref, f32[256,256]{1,0:T(8,128)S(1)} %get-tuple-element.64.near_ref, f32[256,256]{1,0:T(8,128)S(1)} %get-tuple-element.65.mid_ref), custom_call_target="tpu_custom_call" | custom-call | tf_op jit(solution)/shard_map/cond/branch_1_fun/local/pallas_call | solution.py:262
  36.8 1.4 %all-to-all-done = bf16[8,32,128]{2,1,0:T(8,128)(2,1)} async-done(((bf16[8,32,128]{2,1,0:T(8,128)(2,1)S(1)}), bf16[8,32,128]{2,1,0:T(8,128)(2,1)}, u32[]{:S(2)}, u32[]{:S(2)}) %all-to-all-start) | async-done | bytes 65568 | tf_op jit(solution)/shard_map/cond/branch_1_fun/all_to_all | solution.py:247
  38.3 1.3 %collective-permute-start = (bf16[8,32,128]{2,1,0:T(8,128)(2,1)}, bf16[8,32,128]{2,1,0:T(8,128)(2,1)S(1)}, u32[]{:S(2)}, u32[]{:S(2)}) collective-permute-start(bf16[8,32,128]{2,1,0:T(8,128)(2,1)} %get-tuple-element.95), channel_id=1, source_target_pairs={{0,384},{32,416},{64,448},{96,480},{128,352},{160,320},{192,256},{... | collective-permute-start | bytes 196616 | tf_op jit(solution)/shard_map/ppermute | solution.py:309
  39.6 14.9 %conditional.4 = (bf16[32,32,128]{2,1,0:T(8,128)(2,1)S(1)}) conditional(s32[]{:T(128)} %convert_element_type.3, bf16[8,32,128]{2,1,0:T(8,128)(2,1)S(1)} %kept.1, (bf16[32,32,128]{2,1,0:T(8,128)(2,1)S(1)}, s32[2,8]{1,0:T(2,128)S(1)}, f32[16,256]{1,0:T(8,128)S(1)}, f32[4,16,128]{2,1,0:T(8,128)S(1)}, bf16[8,32,128]{2,1,0:T(8,128)(2,1)}) %tuple.27), branch_computations={%region_2.3_spmd, %region_3.4_spmd} | conditional | bytes 1048584 | solution.py:310
  39.6 1.2 %far.2 = bf16[16,2,32,128]{3,2,1,0:T(8,128)(2,1)S(1)} custom-call(s32[2,8]{1,0:T(2,128)S(1)} %get-tuple-element.69.offsets_ref, f32[16,256]{1,0:T(8,128)S(1)} %get-tuple-element.70.bias_ref, f32[4,16,128]{2,1,0:T(8,128)S(1)} %get-tuple-element.71.far_ref, bf16[8,32,128]{2,1,0:T(8,128)(2,1)} %get-tuple-element.72.refs_0_, ...), custom_call_target="tpu_custom_call", output_to_operand_aliasing={{}: (4, {})} | custom-call | tf_op jit(solution)/shard_map/cond/branch_1_fun/far/pallas_call | solution.py:282
  40.9 13.6 %all_to_all.22 = bf16[32,32,128]{2,1,0:T(8,128)(2,1)S(1)} all-to-all(bf16[32,32,128]{2,1,0:T(8,128)(2,1)S(1)} %bitcast.7), channel_id=1, replica_groups={{4,5,6,7,12,13,14,15,20,21,22,23,28,29,30,31,0,1,2,3,8,9,10,11,16,17,18..., dimensions={0} | all-to-all | bytes 524288 | tf_op jit(solution)/shard_map/cond/branch_1_fun/all_to_all | solution.py:291
  54.5 0.0 collective-permute-done
  54.5 0.8 %unpack.1 = bf16[32,4096]{1,0:T(8,128)(2,1)} custom-call(bf16[32,32,128]{2,1,0:T(8,128)(2,1)S(1)} %get-tuple-element.105.in_ref), custom_call_target="tpu_custom_call" | custom-call | tf_op jit(solution)/shard_map/unpack/pallas_call | solution.py:326
  (2 shorter events, 0.0 us)
Async XLA Ops:
  25.6 12.7 %all-to-all-start = ((bf16[8,32,128]{2,1,0:T(8,128)(2,1)S(1)}), bf16[8,32,128]{2,1,0:T(8,128)(2,1)}, u32[]{:S(2)}, u32[]{:S(2)}) async-start(bf16[8,32,128]{2,1,0:T(8,128)(2,1)S(1)} %get-tuple-element.60), calls=%async_computation | async-start | bytes 131072 | tf_op jit(solution)/shard_map/cond/branch_1_fun/all_to_all | solution.py:247
  38.3 16.2 %collective-permute-start = (bf16[8,32,128]{2,1,0:T(8,128)(2,1)}, bf16[8,32,128]{2,1,0:T(8,128)(2,1)S(1)}, u32[]{:S(2)}, u32[]{:S(2)}) collective-permute-start(bf16[8,32,128]{2,1,0:T(8,128)(2,1)} %get-tuple-element.95), channel_id=1, source_target_pairs={{0,384},{32,416},{64,448},{96,480},{128,352},{160,320},{192,256},{... | collective-permute-start | bytes 196616 | tf_op jit(solution)/shard_map/ppermute | solution.py:309

commit v8 on v7

--- a/solution.py
+++ b/solution.py
@@ -24,7 +24,7 @@
 LOW = [6, 0, 1, 2, 3, 4, 5, 7]
 HIGH = [11, 8, 9, 10, 12, 13, 14, 15]
 ORDER_IN = [(2 * y + c) * LANES + x for c in (1, 0) for y in (3, 2, 1, 0) for x in (3, 2, 1, 0)]
-ORDER_OUT = [(2 * y + c) * LANES + x for c in (1, 0) for y in (0, 1, 2, 3) for x in (0, 1, 2, 3)]
+ORDER_OUT = [(2 * y + c) * LANES + x for c in (1, 0) for y in (3, 2, 1, 0) for x in (0, 1, 2, 3)]
 PAIRS_IN = [n // 2 for n in ORDER_IN[::2]]
 PAIRS_OUT = [n // 2 for n in ORDER_OUT[::2]]
 PLACE = {n: p for p, n in enumerate(ORDER_IN)}

time: 55.6 us -> 55.2 us (level)
  no operation moved by 1% of the time
where the time goes in v8:
time: 55.2 us; the launch traced here: 54.9 us
  blocking collectives  37.3 us (68%)
  starting transfers between devices  10.6 us (19%)
  Pallas kernels  5.4 us (10%)
  waiting for transfers between devices  1.43 us (3%)
    all_to_all x1, blocking collectives, on_device(): lax.all_to_all(packed, ('g', 'x'), 0, 0, axis_index_groups=[ORDER_IN], ti...  24.1 us
    all_to_all x1, blocking collectives, finish(): lax.all_to_all(merged.reshape(PEERS, ROWS, DH), ('g', 'x'), 0, 0, axis_in...  13.2 us
    all_to_all x1, starting transfers between devices, exchange(): lax.all_to_all(block, 'z', 0, 0, axis_index_groups=[LOW, HIGH], tiled=True)  9.34 us
    all_to_all x1, waiting for transfers between devices, exchange(): lax.all_to_all(block, 'z', 0, 0, axis_index_groups=[LOW, HIGH], tiled=True)  1.43 us
    ppermute x1, starting transfers between devices, on_device(): lower = lax.ppermute(first, 'z', list(enumerate(UPPER)))  1.28 us
    pallas_call x1, Pallas kernels, on_device(): pl.pallas_call(pack_kernel, out_shape=(jax.ShapeDtypeStruct((PEERS, 3 * R...  1.26 us
    pallas_call x1, Pallas kernels, finish(): pl.pallas_call(far_kernel, out_shape=jax.ShapeDtypeStruct((KEPT, 2, ROWS,...  1.24 us
  transfers between devices with their start and end apart: 2, of which 1 were waited for; matrix products, arithmetic and copies ran while one was open for 0% of the time, Pallas kernels for 6%

profile of v8, /device:TPU:1, one launch (start us, length us, event | category | flops | bytes accessed | tf_op | source)
XLA Modules:
  0.0 54.9 jit_solution(5631057957741927134)
XLA Ops:
  0.0 1.3 %pack.1 = (bf16[32,96,128]{2,1,0:T(8,128)(2,1)S(1)}, s32[2,8]{1,0:T(2,128)S(1)}, f32[8,32]{1,0:T(8,128)S(1)}, bf16[8,32,128]{2,1,0:T(8,128)(2,1)}) custom-call(bf16[32,4096]{1,0:T(8,128)(2,1)} %q_ref.1, bf16[32,4096]{1,0:T(8,128)(2,1)} %k_ref.1, bf16[32,4096]{1,0:T(8,128)(2,1)} %v_ref.1, s32[2,8]{1,0:T(2,128)} %offsets_ref.1, f32[8,32]{1,0:T(8,128)} %bitcast.12, ...), custom_call_target="tpu_custom_call" | custom-call | tf_op jit(solution)/shard_map/pack/pallas_call | solution.py:223
  1.3 24.1 %all_to_all.24 = bf16[32,96,128]{2,1,0:T(8,128)(2,1)S(1)} all-to-all(bf16[32,96,128]{2,1,0:T(8,128)(2,1)S(1)} %get-tuple-element.89), channel_id=1, replica_groups={{31,30,29,28,23,22,21,20,15,14,13,12,7,6,5,4,27,26,25,24,19,18,17,16,11..., dimensions={0} | all-to-all | bytes 1572864 | tf_op jit(solution)/shard_map/all_to_all | solution.py:237
  25.3 0.2 kept.1
  25.6 12.7 %conditional.3 = (bf16[8,32,128]{2,1,0:T(8,128)(2,1)}, bf16[32,32,128]{2,1,0:T(8,128)(2,1)S(1)}, f32[4,16,128]{2,1,0:T(8,128)S(1)}, f32[16,256]{1,0:T(8,128)S(1)}) conditional(s32[]{:T(128)} %convert_element_type.3, (f32[8,32]{1,0:T(8,128)S(1)}, s32[2,8]{1,0:T(2,128)S(1)}, bf16[32,96,128]{2,1,0:T(8,128)(2,1)S(1)}, ...), branch_computations={%region_0.0_spmd, %region_1.0_spmd} | conditional | bytes 196672 | solution.py:300
  25.6 9.3 %all-to-all-start = ((bf16[8,32,128]{2,1,0:T(8,128)(2,1)S(1)}), bf16[8,32,128]{2,1,0:T(8,128)(2,1)}, u32[]{:S(2)}, u32[]{:S(2)}) async-start(bf16[8,32,128]{2,1,0:T(8,128)(2,1)S(1)} %get-tuple-element.60), calls=%async_computation | async-start | bytes 131072 | tf_op jit(solution)/shard_map/cond/branch_1_fun/all_to_all | solution.py:247
  34.9 0.9 %bias.3 = (f32[256,256]{1,0:T(8,128)S(1)}, f32[256,256]{1,0:T(8,128)S(1)}, f32[16,256]{1,0:T(8,128)S(1)}) custom-call(f32[8,32]{1,0:T(8,128)S(1)} %get-tuple-element.63.table_ref), custom_call_target="tpu_custom_call" | custom-call | tf_op jit(solution)/shard_map/cond/branch_1_fun/bias/pallas_call | solution.py:250
  35.8 1.0 %local.3 = (bf16[32,32,128]{2,1,0:T(8,128)(2,1)S(1)}, f32[4,16,128]{2,1,0:T(8,128)S(1)}) custom-call(s32[2,8]{1,0:T(2,128)S(1)} %get-tuple-element.61.offsets_ref, bf16[32,96,128]{2,1,0:T(8,128)(2,1)S(1)} %get-tuple-element.62.qkv_ref, f32[256,256]{1,0:T(8,128)S(1)} %get-tuple-element.64.near_ref, f32[256,256]{1,0:T(8,128)S(1)} %get-tuple-element.65.mid_ref), custom_call_target="tpu_custom_call" | custom-call | tf_op jit(solution)/shard_map/cond/branch_1_fun/local/pallas_call | solution.py:262
  36.8 1.4 %all-to-all-done = bf16[8,32,128]{2,1,0:T(8,128)(2,1)} async-done(((bf16[8,32,128]{2,1,0:T(8,128)(2,1)S(1)}), bf16[8,32,128]{2,1,0:T(8,128)(2,1)}, u32[]{:S(2)}, u32[]{:S(2)}) %all-to-all-start) | async-done | bytes 65568 | tf_op jit(solution)/shard_map/cond/branch_1_fun/all_to_all | solution.py:247
  38.3 1.3 %collective-permute-start = (bf16[8,32,128]{2,1,0:T(8,128)(2,1)}, bf16[8,32,128]{2,1,0:T(8,128)(2,1)S(1)}, u32[]{:S(2)}, u32[]{:S(2)}) collective-permute-start(bf16[8,32,128]{2,1,0:T(8,128)(2,1)} %get-tuple-element.95), channel_id=1, source_target_pairs={{0,384},{32,416},{64,448},{96,480},{128,352},{160,320},{192,256},{... | collective-permute-start | bytes 196616 | tf_op jit(solution)/shard_map/ppermute | solution.py:309
  39.6 14.5 %conditional.4 = (bf16[32,32,128]{2,1,0:T(8,128)(2,1)S(1)}) conditional(s32[]{:T(128)} %convert_element_type.3, bf16[8,32,128]{2,1,0:T(8,128)(2,1)S(1)} %kept.1, (bf16[32,32,128]{2,1,0:T(8,128)(2,1)S(1)}, s32[2,8]{1,0:T(2,128)S(1)}, f32[16,256]{1,0:T(8,128)S(1)}, f32[4,16,128]{2,1,0:T(8,128)S(1)}, bf16[8,32,128]{2,1,0:T(8,128)(2,1)}) %tuple.27), branch_computations={%region_2.3_spmd, %region_3.4_spmd} | conditional | bytes 1048584 | solution.py:310
  39.6 1.2 %far.2 = bf16[16,2,32,128]{3,2,1,0:T(8,128)(2,1)S(1)} custom-call(s32[2,8]{1,0:T(2,128)S(1)} %get-tuple-element.69.offsets_ref, f32[16,256]{1,0:T(8,128)S(1)} %get-tuple-element.70.bias_ref, f32[4,16,128]{2,1,0:T(8,128)S(1)} %get-tuple-element.71.far_ref, bf16[8,32,128]{2,1,0:T(8,128)(2,1)} %get-tuple-element.72.refs_0_, ...), custom_call_target="tpu_custom_call", output_to_operand_aliasing={{}: (4, {})} | custom-call | tf_op jit(solution)/shard_map/cond/branch_1_fun/far/pallas_call | solution.py:282
  40.9 13.2 %all_to_all.22 = bf16[32,32,128]{2,1,0:T(8,128)(2,1)S(1)} all-to-all(bf16[32,32,128]{2,1,0:T(8,128)(2,1)S(1)} %bitcast.7), channel_id=1, replica_groups={{28,29,30,31,20,21,22,23,12,13,14,15,4,5,6,7,24,25,26,27,16,17,18,19,8,..., dimensions={0} | all-to-all | bytes 524288 | tf_op jit(solution)/shard_map/cond/branch_1_fun/all_to_all | solution.py:291
  54.1 0.0 collective-permute-done
  54.1 0.8 %unpack.1 = bf16[32,4096]{1,0:T(8,128)(2,1)} custom-call(bf16[32,32,128]{2,1,0:T(8,128)(2,1)S(1)} %get-tuple-element.105.in_ref), custom_call_target="tpu_custom_call" | custom-call | tf_op jit(solution)/shard_map/unpack/pallas_call | solution.py:326
  (2 shorter events, 0.0 us)
Async XLA Ops:
  25.6 12.7 %all-to-all-start = ((bf16[8,32,128]{2,1,0:T(8,128)(2,1)S(1)}), bf16[8,32,128]{2,1,0:T(8,128)(2,1)}, u32[]{:S(2)}, u32[]{:S(2)}) async-start(bf16[8,32,128]{2,1,0:T(8,128)(2,1)S(1)} %get-tuple-element.60), calls=%async_computation | async-start | bytes 131072 | tf_op jit(solution)/shard_map/cond/branch_1_fun/all_to_all | solution.py:247
  38.3 15.8 %collective-permute-start = (bf16[8,32,128]{2,1,0:T(8,128)(2,1)}, bf16[8,32,128]{2,1,0:T(8,128)(2,1)S(1)}, u32[]{:S(2)}, u32[]{:S(2)}) collective-permute-start(bf16[8,32,128]{2,1,0:T(8,128)(2,1)} %get-tuple-element.95), channel_id=1, source_target_pairs={{0,384},{32,416},{64,448},{96,480},{128,352},{160,320},{192,256},{... | collective-permute-start | bytes 196616 | tf_op jit(solution)/shard_map/ppermute | solution.py:309

commit v9 on v8

--- a/solution.py
+++ b/solution.py
@@ -28,7 +28,7 @@
 PAIRS_IN = [n // 2 for n in ORDER_IN[::2]]
 PAIRS_OUT = [n // 2 for n in ORDER_OUT[::2]]
 PLACE = {n: p for p, n in enumerate(ORDER_IN)}
-UPPER = [12, 13, 14, 15, 11, 10, 8, 9]
+UPPER = [12, 13, 14, 15, 11, 9, 10, 8]
 NEG = -1e30
 SCALE = DH ** (-0.5)
 
@@ -80,10 +80,17 @@
     return jnp.sum(jnp.where(at_row & at_head, values, 0))
 
 
-def unpack_kernel(in_ref, out_ref):
-    for p, n in enumerate(ORDER_OUT):
-        h = GROUPS * (n % LANES) + n // LANES
-        out_ref[:, h * DH : (h + 1) * DH] = in_ref[p]
+def unpack_kernel(in_ref, out_ref, block, sems):
+    copies = []
+    for x in range(LANES):
+        for g in range(GROUPS):
+            h = GROUPS * x + g
+            block[:, h * DH : (h + 1) * DH] = in_ref[ORDER_OUT.index(g * LANES + x)]
+        columns = slice(x * GROUPS * DH, (x + 1) * GROUPS * DH)
+        copies.append(pltpu.make_async_copy(block.at[:, columns], out_ref.at[:, columns], sems.at[x]))
+        copies[-1].start()
+    for copy in copies:
+        copy.wait()
 
 
 def bias_kernel(table_ref, near_ref, mid_ref, far_ref):
@@ -327,7 +334,11 @@
         unpack_kernel,
         out_shape=jax.ShapeDtypeStruct((ROWS, PEERS * DH), bf16),
         in_specs=[VMEM],
-        out_specs=VMEM,
+        out_specs=HBM,
+        scratch_shapes=[
+            pltpu.VMEM((ROWS, PEERS * DH), bf16),
+            pltpu.SemaphoreType.DMA((LANES,)),
+        ],
         compiler_params=params(),
         name="unpack",
     )(back)

time: 55.2 us -> 55.2 us (level)
  no operation moved by 1% of the time
where the time goes in v9:
time: 55.2 us; the launch traced here: 54.8 us
  blocking collectives  37.3 us (68%)
  starting transfers between devices  10.6 us (19%)
  Pallas kernels  5.37 us (10%)
  waiting for transfers between devices  1.43 us (3%)
    all_to_all x1, blocking collectives, on_device(): lax.all_to_all(packed, ('g', 'x'), 0, 0, axis_index_groups=[ORDER_IN], ti...  24.1 us
    all_to_all x1, blocking collectives, finish(): lax.all_to_all(merged.reshape(PEERS, ROWS, DH), ('g', 'x'), 0, 0, axis_in...  13.2 us
    all_to_all x1, starting transfers between devices, exchange(): lax.all_to_all(block, 'z', 0, 0, axis_index_groups=[LOW, HIGH], tiled=True)  9.34 us
    all_to_all x1, waiting for transfers between devices, exchange(): lax.all_to_all(block, 'z', 0, 0, axis_index_groups=[LOW, HIGH], tiled=True)  1.43 us
    ppermute x1, starting transfers between devices, on_device(): lower = lax.ppermute(first, 'z', list(enumerate(UPPER)))  1.28 us
    pallas_call x1, Pallas kernels, on_device(): pl.pallas_call(pack_kernel, out_shape=(jax.ShapeDtypeStruct((PEERS, 3 * R...  1.26 us
    pallas_call x1, Pallas kernels, finish(): pl.pallas_call(far_kernel, out_shape=jax.ShapeDtypeStruct((KEPT, 2, ROWS,...  1.24 us
  transfers between devices with their start and end apart: 2, of which 1 were waited for; matrix products, arithmetic and copies ran while one was open for 0% of the time, Pallas kernels for 6%

profile of v9, /device:TPU:1, one launch (start us, length us, event | category | flops | bytes accessed | tf_op | source)
XLA Modules:
  0.0 54.8 jit_solution(7711625204714520643)
XLA Ops:
  0.0 1.3 %pack.1 = (bf16[32,96,128]{2,1,0:T(8,128)(2,1)S(1)}, s32[2,8]{1,0:T(2,128)S(1)}, f32[8,32]{1,0:T(8,128)S(1)}, bf16[8,32,128]{2,1,0:T(8,128)(2,1)}) custom-call(bf16[32,4096]{1,0:T(8,128)(2,1)} %q_ref.1, bf16[32,4096]{1,0:T(8,128)(2,1)} %k_ref.1, bf16[32,4096]{1,0:T(8,128)(2,1)} %v_ref.1, s32[2,8]{1,0:T(2,128)} %offsets_ref.1, f32[8,32]{1,0:T(8,128)} %bitcast.12, ...), custom_call_target="tpu_custom_call" | custom-call | tf_op jit(solution)/shard_map/pack/pallas_call | solution.py:230
  1.3 24.1 %all_to_all.24 = bf16[32,96,128]{2,1,0:T(8,128)(2,1)S(1)} all-to-all(bf16[32,96,128]{2,1,0:T(8,128)(2,1)S(1)} %get-tuple-element.89), channel_id=1, replica_groups={{31,30,29,28,23,22,21,20,15,14,13,12,7,6,5,4,27,26,25,24,19,18,17,16,11..., dimensions={0} | all-to-all | bytes 1572864 | tf_op jit(solution)/shard_map/all_to_all | solution.py:244
  25.3 0.2 kept.1
  25.6 12.7 %conditional.3 = (bf16[8,32,128]{2,1,0:T(8,128)(2,1)}, bf16[32,32,128]{2,1,0:T(8,128)(2,1)S(1)}, f32[4,16,128]{2,1,0:T(8,128)S(1)}, f32[16,256]{1,0:T(8,128)S(1)}) conditional(s32[]{:T(128)} %convert_element_type.3, (f32[8,32]{1,0:T(8,128)S(1)}, s32[2,8]{1,0:T(2,128)S(1)}, bf16[32,96,128]{2,1,0:T(8,128)(2,1)S(1)}, ...), branch_computations={%region_0.0_spmd, %region_1.0_spmd} | conditional | bytes 196672 | solution.py:307
  25.6 9.3 %all-to-all-start = ((bf16[8,32,128]{2,1,0:T(8,128)(2,1)S(1)}), bf16[8,32,128]{2,1,0:T(8,128)(2,1)}, u32[]{:S(2)}, u32[]{:S(2)}) async-start(bf16[8,32,128]{2,1,0:T(8,128)(2,1)S(1)} %get-tuple-element.60), calls=%async_computation | async-start | bytes 131072 | tf_op jit(solution)/shard_map/cond/branch_1_fun/all_to_all | solution.py:254
  34.9 0.9 %bias.3 = (f32[256,256]{1,0:T(8,128)S(1)}, f32[256,256]{1,0:T(8,128)S(1)}, f32[16,256]{1,0:T(8,128)S(1)}) custom-call(f32[8,32]{1,0:T(8,128)S(1)} %get-tuple-element.63.table_ref), custom_call_target="tpu_custom_call" | custom-call | tf_op jit(solution)/shard_map/cond/branch_1_fun/bias/pallas_call | solution.py:257
  35.8 1.0 %local.3 = (bf16[32,32,128]{2,1,0:T(8,128)(2,1)S(1)}, f32[4,16,128]{2,1,0:T(8,128)S(1)}) custom-call(s32[2,8]{1,0:T(2,128)S(1)} %get-tuple-element.61.offsets_ref, bf16[32,96,128]{2,1,0:T(8,128)(2,1)S(1)} %get-tuple-element.62.qkv_ref, f32[256,256]{1,0:T(8,128)S(1)} %get-tuple-element.64.near_ref, f32[256,256]{1,0:T(8,128)S(1)} %get-tuple-element.65.mid_ref), custom_call_target="tpu_custom_call" | custom-call | tf_op jit(solution)/shard_map/cond/branch_1_fun/local/pallas_call | solution.py:269
  36.8 1.4 %all-to-all-done = bf16[8,32,128]{2,1,0:T(8,128)(2,1)} async-done(((bf16[8,32,128]{2,1,0:T(8,128)(2,1)S(1)}), bf16[8,32,128]{2,1,0:T(8,128)(2,1)}, u32[]{:S(2)}, u32[]{:S(2)}) %all-to-all-start) | async-done | bytes 65568 | tf_op jit(solution)/shard_map/cond/branch_1_fun/all_to_all | solution.py:254
  38.3 1.3 %collective-permute-start = (bf16[8,32,128]{2,1,0:T(8,128)(2,1)}, bf16[8,32,128]{2,1,0:T(8,128)(2,1)S(1)}, u32[]{:S(2)}, u32[]{:S(2)}) collective-permute-start(bf16[8,32,128]{2,1,0:T(8,128)(2,1)} %get-tuple-element.95), channel_id=1, source_target_pairs={{0,384},{32,416},{64,448},{96,480},{128,352},{160,288},{192,320},{... | collective-permute-start | bytes 196616 | tf_op jit(solution)/shard_map/ppermute | solution.py:316
  39.6 14.5 %conditional.4 = (bf16[32,32,128]{2,1,0:T(8,128)(2,1)S(1)}) conditional(s32[]{:T(128)} %convert_element_type.3, bf16[8,32,128]{2,1,0:T(8,128)(2,1)S(1)} %kept.1, (bf16[32,32,128]{2,1,0:T(8,128)(2,1)S(1)}, s32[2,8]{1,0:T(2,128)S(1)}, f32[16,256]{1,0:T(8,128)S(1)}, f32[4,16,128]{2,1,0:T(8,128)S(1)}, bf16[8,32,128]{2,1,0:T(8,128)(2,1)}) %tuple.27), branch_computations={%region_2.3_spmd, %region_3.4_spmd} | conditional | bytes 1048584 | solution.py:317
  39.6 1.2 %far.2 = bf16[16,2,32,128]{3,2,1,0:T(8,128)(2,1)S(1)} custom-call(s32[2,8]{1,0:T(2,128)S(1)} %get-tuple-element.69.offsets_ref, f32[16,256]{1,0:T(8,128)S(1)} %get-tuple-element.70.bias_ref, f32[4,16,128]{2,1,0:T(8,128)S(1)} %get-tuple-element.71.far_ref, bf16[8,32,128]{2,1,0:T(8,128)(2,1)} %get-tuple-element.72.refs_0_, ...), custom_call_target="tpu_custom_call", output_to_operand_aliasing={{}: (4, {})} | custom-call | tf_op jit(solution)/shard_map/cond/branch_1_fun/far/pallas_call | solution.py:289
  40.9 13.2 %all_to_all.22 = bf16[32,32,128]{2,1,0:T(8,128)(2,1)S(1)} all-to-all(bf16[32,32,128]{2,1,0:T(8,128)(2,1)S(1)} %bitcast.7), channel_id=1, replica_groups={{28,29,30,31,20,21,22,23,12,13,14,15,4,5,6,7,24,25,26,27,16,17,18,19,8,..., dimensions={0} | all-to-all | bytes 524288 | tf_op jit(solution)/shard_map/cond/branch_1_fun/all_to_all | solution.py:298
  54.1 0.0 collective-permute-done
  54.1 0.7 %unpack.1 = bf16[32,4096]{1,0:T(8,128)(2,1)} custom-call(bf16[32,32,128]{2,1,0:T(8,128)(2,1)S(1)} %get-tuple-element.105.in_ref), custom_call_target="tpu_custom_call" | custom-call | tf_op jit(solution)/shard_map/unpack/pallas_call | solution.py:333
  (2 shorter events, 0.0 us)
Async XLA Ops:
  25.6 12.7 %all-to-all-start = ((bf16[8,32,128]{2,1,0:T(8,128)(2,1)S(1)}), bf16[8,32,128]{2,1,0:T(8,128)(2,1)}, u32[]{:S(2)}, u32[]{:S(2)}) async-start(bf16[8,32,128]{2,1,0:T(8,128)(2,1)S(1)} %get-tuple-element.60), calls=%async_computation | async-start | bytes 131072 | tf_op jit(solution)/shard_map/cond/branch_1_fun/all_to_all | solution.py:254
  38.3 15.8 %collective-permute-start = (bf16[8,32,128]{2,1,0:T(8,128)(2,1)}, bf16[8,32,128]{2,1,0:T(8,128)(2,1)S(1)}, u32[]{:S(2)}, u32[]{:S(2)}) collective-permute-start(bf16[8,32,128]{2,1,0:T(8,128)(2,1)} %get-tuple-element.95), channel_id=1, source_target_pairs={{0,384},{32,416},{64,448},{96,480},{128,352},{160,288},{192,320},{... | collective-permute-start | bytes 196616 | tf_op jit(solution)/shard_map/ppermute | solution.py:316

commit v10 on v8

--- a/solution.py
+++ b/solution.py
@@ -22,7 +22,7 @@
 KEPT = SEG // R2
 HALF = PLANES // 2
 LOW = [6, 0, 1, 2, 3, 4, 5, 7]
-HIGH = [11, 8, 9, 10, 12, 13, 14, 15]
+HIGH = [10, 8, 9, 11, 12, 13, 14, 15]
 ORDER_IN = [(2 * y + c) * LANES + x for c in (1, 0) for y in (3, 2, 1, 0) for x in (3, 2, 1, 0)]
 ORDER_OUT = [(2 * y + c) * LANES + x for c in (1, 0) for y in (3, 2, 1, 0) for x in (0, 1, 2, 3)]
 PAIRS_IN = [n // 2 for n in ORDER_IN[::2]]

time: 55.2 us -> 55.2 us (level)
  no operation moved by 1% of the time
where the time goes in v10:
time: 55.2 us; the launch traced here: 54.9 us
  blocking collectives  37.3 us (68%)
  starting transfers between devices  10.6 us (19%)
  Pallas kernels  5.4 us (10%)
  waiting for transfers between devices  1.43 us (3%)
    all_to_all x1, blocking collectives, on_device(): lax.all_to_all(packed, ('g', 'x'), 0, 0, axis_index_groups=[ORDER_IN], ti...  24.1 us
    all_to_all x1, blocking collectives, finish(): lax.all_to_all(merged.reshape(PEERS, ROWS, DH), ('g', 'x'), 0, 0, axis_in...  13.2 us
    all_to_all x1, starting transfers between devices, exchange(): lax.all_to_all(block, 'z', 0, 0, axis_index_groups=[LOW, HIGH], tiled=True)  9.34 us
    all_to_all x1, waiting for transfers between devices, exchange(): lax.all_to_all(block, 'z', 0, 0, axis_index_groups=[LOW, HIGH], tiled=True)  1.43 us
    ppermute x1, starting transfers between devices, on_device(): lower = lax.ppermute(first, 'z', list(enumerate(UPPER)))  1.28 us
    pallas_call x1, Pallas kernels, on_device(): pl.pallas_call(pack_kernel, out_shape=(jax.ShapeDtypeStruct((PEERS, 3 * R...  1.26 us
    pallas_call x1, Pallas kernels, finish(): pl.pallas_call(far_kernel, out_shape=jax.ShapeDtypeStruct((KEPT, 2, ROWS,...  1.24 us
  transfers between devices with their start and end apart: 2, of which 1 were waited for; matrix products, arithmetic and copies ran while one was open for 0% of the time, Pallas kernels for 6%

profile of v10, /device:TPU:1, one launch (start us, length us, event | category | flops | bytes accessed | tf_op | source)
XLA Modules:
  0.0 54.9 jit_solution(10604509157831428886)
XLA Ops:
  0.0 1.3 %pack.1 = (bf16[32,96,128]{2,1,0:T(8,128)(2,1)S(1)}, s32[2,8]{1,0:T(2,128)S(1)}, f32[8,32]{1,0:T(8,128)S(1)}, bf16[8,32,128]{2,1,0:T(8,128)(2,1)}) custom-call(bf16[32,4096]{1,0:T(8,128)(2,1)} %q_ref.1, bf16[32,4096]{1,0:T(8,128)(2,1)} %k_ref.1, bf16[32,4096]{1,0:T(8,128)(2,1)} %v_ref.1, s32[2,8]{1,0:T(2,128)} %offsets_ref.1, f32[8,32]{1,0:T(8,128)} %bitcast.12, ...), custom_call_target="tpu_custom_call" | custom-call | tf_op jit(solution)/shard_map/pack/pallas_call | solution.py:223
  1.3 24.1 %all_to_all.24 = bf16[32,96,128]{2,1,0:T(8,128)(2,1)S(1)} all-to-all(bf16[32,96,128]{2,1,0:T(8,128)(2,1)S(1)} %get-tuple-element.89), channel_id=1, replica_groups={{31,30,29,28,23,22,21,20,15,14,13,12,7,6,5,4,27,26,25,24,19,18,17,16,11..., dimensions={0} | all-to-all | bytes 1572864 | tf_op jit(solution)/shard_map/all_to_all | solution.py:237
  25.3 0.2 kept.1
  25.6 12.7 %conditional.3 = (bf16[8,32,128]{2,1,0:T(8,128)(2,1)}, bf16[32,32,128]{2,1,0:T(8,128)(2,1)S(1)}, f32[4,16,128]{2,1,0:T(8,128)S(1)}, f32[16,256]{1,0:T(8,128)S(1)}) conditional(s32[]{:T(128)} %convert_element_type.3, (f32[8,32]{1,0:T(8,128)S(1)}, s32[2,8]{1,0:T(2,128)S(1)}, bf16[32,96,128]{2,1,0:T(8,128)(2,1)S(1)}, ...), branch_computations={%region_0.0_spmd, %region_1.0_spmd} | conditional | bytes 196672 | solution.py:300
  25.6 9.3 %all-to-all-start = ((bf16[8,32,128]{2,1,0:T(8,128)(2,1)S(1)}), bf16[8,32,128]{2,1,0:T(8,128)(2,1)}, u32[]{:S(2)}, u32[]{:S(2)}) async-start(bf16[8,32,128]{2,1,0:T(8,128)(2,1)S(1)} %get-tuple-element.60), calls=%async_computation | async-start | bytes 131072 | tf_op jit(solution)/shard_map/cond/branch_1_fun/all_to_all | solution.py:247
  34.9 0.9 %bias.3 = (f32[256,256]{1,0:T(8,128)S(1)}, f32[256,256]{1,0:T(8,128)S(1)}, f32[16,256]{1,0:T(8,128)S(1)}) custom-call(f32[8,32]{1,0:T(8,128)S(1)} %get-tuple-element.63.table_ref), custom_call_target="tpu_custom_call" | custom-call | tf_op jit(solution)/shard_map/cond/branch_1_fun/bias/pallas_call | solution.py:250
  35.8 1.0 %local.3 = (bf16[32,32,128]{2,1,0:T(8,128)(2,1)S(1)}, f32[4,16,128]{2,1,0:T(8,128)S(1)}) custom-call(s32[2,8]{1,0:T(2,128)S(1)} %get-tuple-element.61.offsets_ref, bf16[32,96,128]{2,1,0:T(8,128)(2,1)S(1)} %get-tuple-element.62.qkv_ref, f32[256,256]{1,0:T(8,128)S(1)} %get-tuple-element.64.near_ref, f32[256,256]{1,0:T(8,128)S(1)} %get-tuple-element.65.mid_ref), custom_call_target="tpu_custom_call" | custom-call | tf_op jit(solution)/shard_map/cond/branch_1_fun/local/pallas_call | solution.py:262
  36.8 1.4 %all-to-all-done = bf16[8,32,128]{2,1,0:T(8,128)(2,1)} async-done(((bf16[8,32,128]{2,1,0:T(8,128)(2,1)S(1)}), bf16[8,32,128]{2,1,0:T(8,128)(2,1)}, u32[]{:S(2)}, u32[]{:S(2)}) %all-to-all-start) | async-done | bytes 65568 | tf_op jit(solution)/shard_map/cond/branch_1_fun/all_to_all | solution.py:247
  38.3 1.3 %collective-permute-start = (bf16[8,32,128]{2,1,0:T(8,128)(2,1)}, bf16[8,32,128]{2,1,0:T(8,128)(2,1)S(1)}, u32[]{:S(2)}, u32[]{:S(2)}) collective-permute-start(bf16[8,32,128]{2,1,0:T(8,128)(2,1)} %get-tuple-element.95), channel_id=1, source_target_pairs={{0,384},{32,416},{64,448},{96,480},{128,352},{160,320},{192,256},{... | collective-permute-start | bytes 196616 | tf_op jit(solution)/shard_map/ppermute | solution.py:309
  39.6 14.5 %conditional.4 = (bf16[32,32,128]{2,1,0:T(8,128)(2,1)S(1)}) conditional(s32[]{:T(128)} %convert_element_type.3, bf16[8,32,128]{2,1,0:T(8,128)(2,1)S(1)} %kept.1, (bf16[32,32,128]{2,1,0:T(8,128)(2,1)S(1)}, s32[2,8]{1,0:T(2,128)S(1)}, f32[16,256]{1,0:T(8,128)S(1)}, f32[4,16,128]{2,1,0:T(8,128)S(1)}, bf16[8,32,128]{2,1,0:T(8,128)(2,1)}) %tuple.27), branch_computations={%region_2.3_spmd, %region_3.4_spmd} | conditional | bytes 1048584 | solution.py:310
  39.6 1.2 %far.2 = bf16[16,2,32,128]{3,2,1,0:T(8,128)(2,1)S(1)} custom-call(s32[2,8]{1,0:T(2,128)S(1)} %get-tuple-element.69.offsets_ref, f32[16,256]{1,0:T(8,128)S(1)} %get-tuple-element.70.bias_ref, f32[4,16,128]{2,1,0:T(8,128)S(1)} %get-tuple-element.71.far_ref, bf16[8,32,128]{2,1,0:T(8,128)(2,1)} %get-tuple-element.72.refs_0_, ...), custom_call_target="tpu_custom_call", output_to_operand_aliasing={{}: (4, {})} | custom-call | tf_op jit(solution)/shard_map/cond/branch_1_fun/far/pallas_call | solution.py:282
  40.9 13.2 %all_to_all.22 = bf16[32,32,128]{2,1,0:T(8,128)(2,1)S(1)} all-to-all(bf16[32,32,128]{2,1,0:T(8,128)(2,1)S(1)} %bitcast.7), channel_id=1, replica_groups={{28,29,30,31,20,21,22,23,12,13,14,15,4,5,6,7,24,25,26,27,16,17,18,19,8,..., dimensions={0} | all-to-all | bytes 524288 | tf_op jit(solution)/shard_map/cond/branch_1_fun/all_to_all | solution.py:291
  54.1 0.0 collective-permute-done
  54.1 0.8 %unpack.1 = bf16[32,4096]{1,0:T(8,128)(2,1)} custom-call(bf16[32,32,128]{2,1,0:T(8,128)(2,1)S(1)} %get-tuple-element.105.in_ref), custom_call_target="tpu_custom_call" | custom-call | tf_op jit(solution)/shard_map/unpack/pallas_call | solution.py:326
  (2 shorter events, 0.0 us)
Async XLA Ops:
  25.6 12.7 %all-to-all-start = ((bf16[8,32,128]{2,1,0:T(8,128)(2,1)S(1)}), bf16[8,32,128]{2,1,0:T(8,128)(2,1)}, u32[]{:S(2)}, u32[]{:S(2)}) async-start(bf16[8,32,128]{2,1,0:T(8,128)(2,1)S(1)} %get-tuple-element.60), calls=%async_computation | async-start | bytes 131072 | tf_op jit(solution)/shard_map/cond/branch_1_fun/all_to_all | solution.py:247
  38.3 15.8 %collective-permute-start = (bf16[8,32,128]{2,1,0:T(8,128)(2,1)}, bf16[8,32,128]{2,1,0:T(8,128)(2,1)S(1)}, u32[]{:S(2)}, u32[]{:S(2)}) collective-permute-start(bf16[8,32,128]{2,1,0:T(8,128)(2,1)} %get-tuple-element.95), channel_id=1, source_target_pairs={{0,384},{32,416},{64,448},{96,480},{128,352},{160,320},{192,256},{... | collective-permute-start | bytes 196616 | tf_op jit(solution)/shard_map/ppermute | solution.py:309
